TPU v7x, 32 devices: a whole 2x2x4 slice. The times are simulated.
32 devices in a mesh: rep: 8 (over z, core), exp: 4 (over y, x).
Axes of the slice: x: 2, y: 2, z: 4, core: 2. Of those that a mesh axis runs over, the one named last changes fastest.
Arguments:
- tokens: bfloat16 [4096, 4096], P(('rep', 'exp')), may hold values from -6 to 6
- grad_out: bfloat16 [4096, 4096], P(('rep', 'exp')), may hold values from -6 to 6
- gates: float32 [4096, 2], P(('rep', 'exp')), may hold values from 0.1 to 0.9
- expert_ids: int32 [4096, 2], P(('rep', 'exp')), may hold values from 0 to 3, all different within a row; in each aligned block of 128 rows (0 to 127, 128 to 255, ...) at most 80 rows name the same one
- w_all: bfloat16 [4, 4096, 384], P('exp', 'rep'), may hold values from -0.09375 to 0.09375
- touched: int32 [8, 4, 32], P('rep', 'exp'), may hold values 0 or 1
Outputs:
- token_grad: bfloat16 [4096, 4096], P(('rep', 'exp'))
- weight_grad: float32 [4, 4096, 384], P('exp', 'rep')
Inputs may be any that keep to these rules, and one draw needn't show every extreme that they name: `expert_ids`: each token names two different experts. Among the tokens of one device no expert is named more than 80 times, a bound that some block reaches.
All inputs are finite; a program needn't handle non-finite values. No bound on the sum of `touched` on one device may be relied on, other than what follows from the above.
Results may differ from a plain program's by a relative error of at most 0.017.
Values may be sent and summed in bfloat16 or wider, within the bound.
A program may use at most 64 MiB of HBM per device.

v0:
```python
import jax
import jax.numpy as jnp
from jax import lax
from jax.sharding import PartitionSpec as P


def silu_terms(gate_pre):
    sigmoid_g = jax.nn.sigmoid(gate_pre)
    return (gate_pre * sigmoid_g, sigmoid_g * (1.0 + gate_pre * (1.0 - sigmoid_g)))


def contract_rows(left, right):
    return lax.dot_general(
        left, right, (((0,), (0,)), ((), ())), preferred_element_type=jnp.float32
    )


def per_device(tokens, grad_out, gates, expert_ids, w_all, touched):
    tok_count = tokens.shape[0]
    model_width = tokens.shape[1]
    expert_count = lax.axis_size("exp")
    capacity = 5 * tok_count // (2 * expert_count)
    slot_count = expert_count * capacity
    hidden_count = w_all.shape[2] // 3
    flat_ids = expert_ids.reshape(-1)
    onehot = (flat_ids[:, None] == jnp.arange(expert_count, dtype=jnp.int32)[None, :]).astype(
        jnp.int32
    )
    slot_rank = jnp.sum(jnp.cumsum(onehot, 0) * onehot, 1) - 1
    target = flat_ids * capacity + slot_rank
    placed = target[None, :] == jnp.arange(slot_count, dtype=jnp.int32)[:, None]
    place_pair = placed.astype(jnp.bfloat16)
    place_token = jnp.sum(placed.reshape(slot_count, tok_count, 2).astype(jnp.int32), 2).astype(
        jnp.bfloat16
    )
    scaled = (grad_out.astype(jnp.float32)[:, None, :] * gates[:, :, None]).astype(jnp.bfloat16)
    scaled = scaled.reshape(2 * tok_count, model_width)
    send_x = jnp.dot(place_token, tokens, preferred_element_type=jnp.float32).astype(jnp.bfloat16)
    send_dy = jnp.dot(place_pair, scaled, preferred_element_type=jnp.float32).astype(jnp.bfloat16)
    recv_x, recv_dy = (
        lax.all_to_all(
            send_x.reshape(expert_count, capacity, model_width),
            "exp",
            split_axis=0,
            concat_axis=0,
            tiled=True,
        ),
        lax.all_to_all(
            send_dy.reshape(expert_count, capacity, model_width),
            "exp",
            split_axis=0,
            concat_axis=0,
            tiled=True,
        ),
    )
    slot_x = recv_x.reshape(slot_count, model_width)
    slot_dy = recv_dy.reshape(slot_count, model_width)
    w_local = w_all[0]
    shard_rows = lax.all_gather(w_local, "rep", axis=0, tiled=True)
    gate_up = jnp.dot(slot_x, shard_rows[:, : 2 * hidden_count], preferred_element_type=jnp.float32)
    hid_grad = jnp.dot(
        slot_dy, shard_rows[:, 2 * hidden_count :], preferred_element_type=jnp.float32
    )
    gate_pre = gate_up[:, :hidden_count]
    up_pre = gate_up[:, hidden_count:]
    silu_val, silu_slope = silu_terms(gate_pre)
    hidden = (silu_val * up_pre).astype(jnp.bfloat16)
    gate_grad = (hid_grad * up_pre * silu_slope).astype(jnp.bfloat16)
    up_grad = (hid_grad * silu_val).astype(jnp.bfloat16)
    both_grad = jnp.concatenate([gate_grad, up_grad], 1)
    row_mask = jnp.repeat(touched[0, 0].astype(jnp.float32), 128)[:, None]
    full_grad = jnp.concatenate(
        [contract_rows(slot_x, both_grad), contract_rows(slot_dy, hidden)], 1
    )
    masked = lax.optimization_barrier((full_grad * row_mask).astype(jnp.bfloat16)).astype(
        jnp.float32
    )
    owned = lax.psum_scatter(
        masked.astype(jnp.bfloat16), "rep", scatter_dimension=0, tiled=True
    ).astype(jnp.float32)
    slot_grad = lax.dot_general(
        both_grad,
        lax.all_gather(w_local[:, : 2 * hidden_count], "rep", axis=0, tiled=True),
        (((1,), (1,)), ((), ())),
        preferred_element_type=jnp.float32,
    )
    slot_grad = slot_grad.astype(jnp.bfloat16)
    returned = lax.all_to_all(
        slot_grad.reshape(expert_count, capacity, model_width),
        "exp",
        split_axis=0,
        concat_axis=0,
        tiled=True,
    )
    returned = returned.reshape(slot_count, model_width)
    token_grad = contract_rows(place_token, returned).astype(jnp.bfloat16)
    return (token_grad, owned[None])


def solution(mesh):
    in_specs = (
        P(("rep", "exp"), None),
        P(("rep", "exp"), None),
        P(("rep", "exp"), None),
        P(("rep", "exp"), None),
        P("exp", "rep", None),
        P("rep", "exp", None),
    )
    out_specs = (P(("rep", "exp"), None), P("exp", "rep", None))
    return jax.shard_map(
        per_device, mesh=mesh, in_specs=in_specs, out_specs=out_specs, check_vma=False
    )
```

profile of v0, /device:TPU:0, one launch (start us, length us, event | category | flops | bytes accessed | tf_op | source)
XLA Modules:
  0.0 145.9 jit_solution(8583746752603478785)
XLA Ops:
  7.2 0.7 all-gather.6.cloned.1.call-update
  7.9 0.8 copy.29
  9.0 1.2 reduce-window.6
  10.8 0.7 multiply_add_fusion.1
  11.6 2.3 %convolution_convert_fusion.1 = bf16[320,4096]{1,0:T(8,128)(2,1)} fusion(bf16[128,4096]{1,0:T(8,128)(2,1)S(1)} %copy-done, s32[320,128]{1,0:T(8,128)S(1)} %convert_reduce_fusion), kind=kOutput, calls=%fused_computation.3 | convolution fusion | flops 336896000 | bytes 3833856 | tf_op jit(solution)/shard_map/dot_general | solution.py:38
  13.9 5.3 %all-to-all-start.1 = ((bf16[4,80,4096]{2,1,0:T(8,128)(2,1)}), bf16[4,80,4096]{2,1,0:T(8,128)(2,1)}, u32[]{:S(2)}, u32[]{:S(2)}) async-start(bf16[4,80,4096]{2,1,0:T(8,128)(2,1)} %bitcast.38), calls=%async_computation.1 | async-start | bytes 5242880 | tf_op jit(solution)/shard_map/all_to_all | solution.py:41
  19.2 4.1 %mul.72 = f32[128,2,4096]{2,1,0:T(2,128)} broadcast(bf16[128,4096]{1,0:T(8,128)(2,1)S(1)} %copy-done.2), dimensions={0,2} | broadcast | bytes 5242880 | tf_op jit(solution)/shard_map/mul | solution.py:36
  23.3 6.1 %mul.73 = f32[256,4096]{1,0:T(8,128)} reshape(f32[128,2,4096]{2,1,0:T(2,128)} %mul.72) | data formatting | bytes 8388608 | tf_op jit(solution)/shard_map/mul | solution.py:36
  29.6 4.7 %convolution_convert_fusion.2 = bf16[320,4096]{1,0:T(8,128)(2,1)} fusion(f32[256,4096]{1,0:T(8,128)} %mul.73, f32[256]{0:T(256)S(1)} %mul.74, s32[256]{0:T(256)S(1)} %get-tuple-element.13), kind=kOutput, calls=%fused_computation.4 | convolution fusion | flops 674578432 | bytes 6817792 | tf_op jit(solution)/shard_map/dot_general | solution.py:39
  34.3 16.4 %all-to-all-done.1 = bf16[4,80,4096]{2,1,0:T(8,128)(2,1)} async-done(((bf16[4,80,4096]{2,1,0:T(8,128)(2,1)}), bf16[4,80,4096]{2,1,0:T(8,128)(2,1)}, u32[]{:S(2)}, u32[]{:S(2)}) %all-to-all-start.1) | async-done | bytes 2621472 | tf_op jit(solution)/shard_map/all_to_all | solution.py:41
  50.7 4.7 %all-to-all-start = ((bf16[4,80,4096]{2,1,0:T(8,128)(2,1)}), bf16[4,80,4096]{2,1,0:T(8,128)(2,1)}, u32[]{:S(2)}, u32[]{:S(2)}) async-start(bf16[4,80,4096]{2,1,0:T(8,128)(2,1)} %bitcast.37), calls=%async_computation | async-start | bytes 5242880 | tf_op jit(solution)/shard_map/all_to_all | solution.py:48
  55.5 0.7 slice.33
  56.3 3.2 %fusion.1 = f32[320,256]{1,0:T(8,128)S(1)} fusion(bf16[320,4096]{1,0:T(8,128)(2,1)} %bitcast.6, bf16[4096,384]{1,0:T(8,128)(2,1)} %bitcast.43), kind=kOutput, calls=%fused_computation.7 | convolution fusion | flops 671088640 | bytes 5046272 | tf_op jit(solution)/shard_map/dot_general | solution.py:60
  59.6 26.1 %all-to-all-done = bf16[4,80,4096]{2,1,0:T(8,128)(2,1)} async-done(((bf16[4,80,4096]{2,1,0:T(8,128)(2,1)}), bf16[4,80,4096]{2,1,0:T(8,128)(2,1)}, u32[]{:S(2)}, u32[]{:S(2)}) %all-to-all-start) | async-done | bytes 2621472 | tf_op jit(solution)/shard_map/all_to_all | solution.py:48
  85.7 2.9 %multiply_convert_fusion.4 = (bf16[320,128]{1,0:T(8,128)(2,1)S(1)}, bf16[320,128]{1,0:T(8,128)(2,1)S(1)}) fusion(f32[320,256]{1,0:T(8,128)S(1)} %fusion.1, bf16[320,4096]{1,0:T(8,128)(2,1)} %bitcast.3, bf16[4096,384]{1,0:T(8,128)(2,1)} %bitcast.44), kind=kOutput, calls=%fused_computation.19 | convolution fusion | flops 336076800 | bytes 4161536 | tf_op jit(solution)/shard_map/dot_general | solution.py:61
  88.6 2.5 %fusion.9 = f32[4096,128]{0,1:T(8,128)S(1)} fusion(bf16[320,4096]{1,0:T(8,128)(2,1)} %bitcast.3, f32[320,256]{1,0:T(8,128)S(1)} %fusion.1), kind=kOutput, calls=%fused_computation.24 | convolution fusion | flops 335790080 | bytes 5046272 | tf_op jit(solution)/shard_map/dot_general | solution.py:13
  91.1 3.0 %fusion.8 = f32[4096,256]{0,1:T(8,128)S(1)} fusion(bf16[320,4096]{1,0:T(8,128)(2,1)} %bitcast.6, bf16[320,128]{1,0:T(8,128)(2,1)S(1)} %get-tuple-element.11, bf16[320,128]{1,0:T(8,128)(2,1)S(1)} %get-tuple-element.10), kind=kOutput, calls=%fused_computation.23 | convolution fusion | flops 671416320 | bytes 6979584 | tf_op jit(solution)/shard_map/dot_general | solution.py:13
  94.1 2.3 %fusion = bf16[4096,384]{0,1:T(8,128)(2,1)} fusion(f32[4096,128]{0,1:T(8,128)S(1)} %fusion.9, f32[4096,256]{0,1:T(8,128)S(1)} %fusion.8, f32[4096]{0:T(1024)S(1)} %broadcast_bitcast_fusion), kind=kLoop, calls=%fused_computation.1 | loop fusion | flops 4718592 | bytes 9453568 | tf_op jit(solution)/shard_map/convert_element_type | solution.py:75
  96.5 2.5 %convolution_convert_fusion = bf16[320,4096]{1,0:T(8,128)(2,1)S(1)} fusion(bf16[4096,256]{1,0:T(8,128)(2,1)} %all-gather.4.cloned.1.call-done, bf16[320,128]{1,0:T(8,128)(2,1)S(1)} %get-tuple-element.11, bf16[320,128]{1,0:T(8,128)(2,1)S(1)} %get-tuple-element.10), kind=kOutput, calls=%fused_computation.2 | convolution fusion | flops 672727040 | bytes 4882432 | tf_op jit(solution)/shard_map/dot_general | solution.py:81
  99.0 32.9 %all_to_all.15 = bf16[4,80,4096]{2,1,0:T(8,128)(2,1)S(1)} all-to-all(bf16[4,80,4096]{2,1,0:T(8,128)(2,1)S(1)} %bitcast.39), channel_id=1, replica_groups=mesh['rep'=8,'exp'=4] {'exp'}, dimensions={0} | all-to-all | bytes 5242880 | tf_op jit(solution)/shard_map/all_to_all | solution.py:88
  131.9 1.7 %convolution_convert_fusion.3 = bf16[128,4096]{1,0:T(8,128)(2,1)} fusion(bf16[320,4096]{1,0:T(8,128)(2,1)S(1)} %bitcast.40, s32[320,128]{1,0:T(8,128)S(1)} %convert_reduce_fusion), kind=kOutput, calls=%fused_computation.5 | convolution fusion | flops 336109568 | bytes 3833856 | tf_op jit(solution)/shard_map/dot_general | solution.py:13
  133.6 3.5 %reduce-scatter.2.cloned.1.call-done = bf16[512,384]{0,1:T(8,128)(2,1)} async-done(((bf16[4096,384]{0,1:T(8,128)(2,1)}), bf16[512,384]{0,1:T(8,128)(2,1)}) %reduce-scatter.2.cloned.1.call-update) | async-done | bytes 393232 | tf_op jit(solution)/shard_map/reduce_scatter | solution.py:78
  137.2 1.1 bitcast_convert_fusion
  138.3 1.2 copy.35
  (35 shorter events, 1.5 us)
Async XLA Ops:
  7.2 4.4 %copy-start = (bf16[128,4096]{1,0:T(8,128)(2,1)S(1)}, bf16[128,4096]{1,0:T(8,128)(2,1)}, u32[]{:S(2)}) copy-start(bf16[128,4096]{1,0:T(8,128)(2,1)} %param.6) | copy-start | bytes 3145732
  7.2 49.2 %all-gather.6.cloned.1.call-start = ((), (), s32[]{:S(2)}) async-start(), calls=%async_computation.6 | async-start | bytes 3538944 | tf_op jit(solution)/shard_map/all_gather | solution.py:59
  13.9 5.3 %copy-start.2 = (bf16[128,4096]{1,0:T(8,128)(2,1)S(1)}, bf16[128,4096]{1,0:T(8,128)(2,1)}, u32[]{:S(2)}) copy-start(bf16[128,4096]{1,0:T(8,128)(2,1)} %param.7) | copy-start | bytes 3145732
  13.9 36.8 %all-to-all-start.1 = ((bf16[4,80,4096]{2,1,0:T(8,128)(2,1)}), bf16[4,80,4096]{2,1,0:T(8,128)(2,1)}, u32[]{:S(2)}, u32[]{:S(2)}) async-start(bf16[4,80,4096]{2,1,0:T(8,128)(2,1)} %bitcast.38), calls=%async_computation.1 | async-start | bytes 5242880 | tf_op jit(solution)/shard_map/all_to_all | solution.py:41
  23.3 6.1 %copy-start.3 = (f32[128,2]{0,1:T(2,128)S(1)}, f32[128,2]{0,1:T(2,128)}, u32[]{:S(2)}) copy-start(f32[128,2]{0,1:T(2,128)} %param.8) | copy-start | bytes 3076
  50.7 4.7 %copy-start.1 = (bf16[1,512,384]{2,1,0:T(8,128)(2,1)S(1)}, bf16[1,512,384]{2,1,0:T(8,128)(2,1)}, u32[]{:S(2)}) copy-start(bf16[1,512,384]{2,1,0:T(8,128)(2,1)} %param.10) | copy-start | bytes 1179652
  50.7 5.5 %copy-start.4 = (s32[1,1,32]{2,1,0:T(1,128)S(1)}, s32[1,1,32]{2,1,0:T(1,128)}, u32[]{:S(2)}) copy-start(s32[1,1,32]{2,1,0:T(1,128)} %param.11) | copy-start | bytes 388
  50.7 35.0 %all-to-all-start = ((bf16[4,80,4096]{2,1,0:T(8,128)(2,1)}), bf16[4,80,4096]{2,1,0:T(8,128)(2,1)}, u32[]{:S(2)}, u32[]{:S(2)}) async-start(bf16[4,80,4096]{2,1,0:T(8,128)(2,1)} %bitcast.37), calls=%async_computation | async-start | bytes 5242880 | tf_op jit(solution)/shard_map/all_to_all | solution.py:48
  55.4 41.1 %all-gather.4.cloned.1.call-start = ((), (), s32[]{:S(2)}) async-start(), calls=%async_computation.4 | async-start | bytes 2359296 | tf_op jit(solution)/shard_map/all_gather | solution.py:83
  56.2 81.0 %reduce-scatter.2.cloned.1.call-start = ((), (), s32[]{:S(2)}) async-start(), calls=%async_computation.5 | async-start | bytes 3538944 | tf_op jit(solution)/shard_map/reduce_scatter | solution.py:78
Sparse Core Ops, SparseCore 0:
  9.7 40.9 all-gather.5
  58.4 30.9 all-gather.3
  96.6 40.5 reduce-scatter.1
where the time goes:
time: 147 us; the launch traced here: 146 us
  waiting for transfers between devices  46.8 us (32%)
  blocking collectives  32.9 us (22%)
  matrix products  22.8 us (16%)
  local copies, waits for them, and re-layouts  13.9 us (9%)
  between operations  13.9 us (9%)
  starting transfers between devices  10.1 us (7%)
  other arithmetic  5.51 us (4%)
    all_to_all x1, blocking collectives, per_device(): lax.all_to_all(slot_grad.reshape(expert_count, capacity, model_width), 'e...  32.9 us
    all_to_all x1, waiting for transfers between devices, per_device(): lax.all_to_all(send_dy.reshape(expert_count, capacity, model_width), 'exp...  26.1 us
    all_to_all x1, waiting for transfers between devices, per_device(): lax.all_to_all(send_x.reshape(expert_count, capacity, model_width), 'exp'...  16.4 us
    mul x3, local copies, waits for them, and re-layouts, per_device(): grad_out.astype(jnp.float32)[:, None, :] * gates[:, :, None]  10.3 us
    dot_general x3, matrix products, contract_rows(): lax.dot_general(left, right, (((0,), (0,)), ((), ())), preferred_element_...  7.28 us
    all_to_all x1, starting transfers between devices, per_device(): lax.all_to_all(send_x.reshape(expert_count, capacity, model_width), 'exp'...  5.3 us
    all_to_all x1, starting transfers between devices, per_device(): lax.all_to_all(send_dy.reshape(expert_count, capacity, model_width), 'exp...  4.68 us
    dot_general x1, matrix products, per_device(): jnp.dot(place_pair, scaled, preferred_element_type=jnp.float32)  4.67 us
  transfers between devices with their start and end apart: 5, of which 3 were waited for; matrix products, arithmetic and copies ran while one was open for 27% of the time, Pallas kernels for 0%

commit v1 on v0

--- a/solution.py
+++ b/solution.py
@@ -1,7 +1,14 @@
+import functools
 import jax
 import jax.numpy as jnp
 from jax import lax
+from jax.experimental import pallas as pl
+from jax.experimental.pallas import tpu as pltpu
 from jax.sharding import PartitionSpec as P
+
+MESH = pl.DeviceIdType.MESH
+BF16 = jnp.bfloat16
+F32 = jnp.float32
 
 
 def silu_terms(gate_pre):
@@ -15,7 +22,394 @@
     )
 
 
-def per_device(tokens, grad_out, gates, expert_ids, w_all, touched):
+def kernel(
+    R, E, T, S, H,
+    x_ref, g_ref, w_ref, id_ref, tm_ref, gate_ref,
+    dx_out, dw_out,
+    X, Y, IDS, TM, W, ACC, PS, PR, AA, GU, HD, DX, DW, SB, UP, DN, FS, FW,
+    a2s, a2r, wr, ws, bs, br, us, ur, loc,
+):
+    H2, H3 = 2 * H, 3 * H
+    Z = R // 2
+    r = lax.axis_index("rep")
+    q = lax.axis_index("exp")
+    z, c = r // 2, lax.rem(r, 2)
+    sib = (2 * z + 1 - c, q)
+    above = (lax.rem(r + 2, R), q)
+    below = (lax.rem(r + R - 2, R), q)
+    has_up, has_dn = z < Z - 1, z > 0
+
+    barrier = pltpu.get_barrier_semaphore()
+    for j in range(1, E):
+        pl.semaphore_signal(barrier, inc=1, device_id=(r, lax.rem(q + j, E)), device_id_type=MESH)
+    pl.semaphore_signal(barrier, inc=1, device_id=sib, device_id_type=MESH)
+
+    @pl.when(has_up)
+    def _():
+        pl.semaphore_signal(barrier, inc=1, device_id=above, device_id_type=MESH)
+
+    @pl.when(has_dn)
+    def _():
+        pl.semaphore_signal(barrier, inc=1, device_id=below, device_id_type=MESH)
+
+    edge = jnp.where(z == 0, 1, 0) + jnp.where(z == Z - 1, 1, 0)
+    pl.semaphore_wait(barrier, E + 2 - edge)
+
+    def rcopy(src, dst, ss, rs, dev):
+        return pltpu.make_async_remote_copy(
+            src_ref=src, dst_ref=dst, send_sem=ss, recv_sem=rs, device_id=dev, device_id_type=MESH
+        )
+
+    def peer(j):
+        return lax.rem(q + j, E)
+
+    def put(kind, j, src, dst):
+        return rcopy(src, dst, a2s.at[kind, j], a2r.at[kind, q], (r, peer(j)))
+
+    def got(kind, j, dst):
+        p = peer(j)
+        rcopy(dst.at[p], dst.at[p], a2s.at[kind, j], a2r.at[kind, p], (r, p)).wait_recv()
+
+    sent = []
+
+    def start(kind, j, src, dst):
+        d = put(kind, j, src, dst)
+        d.start()
+        sent.append(d)
+
+    WR = W.at[r]
+    for j in range(1, E):
+        start(0, j, w_ref.at[peer(j)], WR.at[q])
+    for j in range(1, E):
+        start(1, j, id_ref, IDS.at[q])
+        start(2, j, tm_ref.at[peer(j)], TM.at[q])
+    for j in range(1, E):
+        start(3, j, x_ref.at[peer(j)], X.at[q])
+    for j in range(1, E):
+        start(4, j, g_ref.at[peer(j)], Y.at[q])
+    WR[q] = w_ref[q]
+    IDS[q] = id_ref[...]
+    TM[q] = tm_ref[q]
+    X[q] = x_ref[q]
+    Y[q] = g_ref[q]
+    ACC[...] = jnp.zeros_like(ACC)
+    for j in range(1, E):
+        got(0, j, WR)
+
+    def w_up(zz):
+        s = 2 * zz + c
+        return rcopy(W.at[s], W.at[s], ws.at[0, zz], wr.at[s], above)
+
+    def w_dn(zz):
+        s = 2 * zz + c
+        return rcopy(W.at[s], W.at[s], ws.at[1, zz], wr.at[s], below)
+
+    def w_sib(zz):
+        s = 2 * zz + c
+        return rcopy(W.at[s], W.at[s], ws.at[2, zz], wr.at[s], sib)
+
+    def w_wait(s):
+        rcopy(W.at[s], W.at[s], ws.at[0, 0], wr.at[s], sib).wait_recv()
+
+    def project(s):
+        xs = X[:, s].reshape(E * T, S)
+        ys = Y[:, s].reshape(E * T, S)
+        for e in range(E):
+            ACC[:, e * H3 : e * H3 + H2] += jnp.dot(
+                xs, W[s, e, :, :H2], preferred_element_type=F32
+            )
+            ACC[:, e * H3 + H2 : (e + 1) * H3] += jnp.dot(
+                ys, W[s, e, :, H2:], preferred_element_type=F32
+            )
+
+    @pl.when(has_up)
+    def _():
+        w_up(z).start()
+
+    @pl.when(has_dn)
+    def _():
+        w_dn(z).start()
+
+    w_sib(z).start()
+    for j in range(1, E):
+        got(1, j, IDS)
+        got(2, j, TM)
+    for j in range(1, E):
+        got(3, j, X)
+    for j in range(1, E):
+        got(4, j, Y)
+    project(r)
+    w_wait(2 * z + 1 - c)
+    project(2 * z + 1 - c)
+    for d in range(1, Z):
+        lo, hi = z - d, z + d
+        has_lo, has_hi = lo >= 0, hi < Z
+
+        @pl.when(has_lo)
+        def _():
+            w_wait(2 * lo + c)
+
+            @pl.when(has_up)
+            def _():
+                w_up(lo).start()
+
+            w_sib(lo).start()
+
+        @pl.when(has_hi)
+        def _():
+            w_wait(2 * hi + c)
+
+            @pl.when(has_dn)
+            def _():
+                w_dn(hi).start()
+
+            w_sib(hi).start()
+
+        @pl.when(has_lo)
+        def _():
+            project(2 * lo + c)
+            w_wait(2 * lo + 1 - c)
+            project(2 * lo + 1 - c)
+
+        @pl.when(has_hi)
+        def _():
+            project(2 * hi + c)
+            w_wait(2 * hi + 1 - c)
+            project(2 * hi + 1 - c)
+
+    for j in list(range(1, E)) + [0]:
+        p = peer(j)
+        ids = IDS[p].astype(F32)
+        rows = pl.ds(pl.multiple_of(p * T, T), T)
+        for k in range(2):
+            tot = jnp.zeros((T, H3), F32)
+            for e in range(E):
+                m = (ids[:, k : k + 1] == e).astype(F32)
+                tot = tot + m * ACC[rows, e * H3 : (e + 1) * H3]
+            PS[p, :, k * H3 : (k + 1) * H3] = tot.astype(BF16)
+        if j:
+            start(5, j, PS.at[p], PR.at[q])
+    for j in range(1, E):
+        got(5, j, PR)
+    for k in range(2):
+        tot = PS[q, :, k * H3 : (k + 1) * H3].astype(F32)
+        for j in range(1, E):
+            tot = tot + PR[peer(j), :, k * H3 : (k + 1) * H3].astype(F32)
+        gate = gate_ref[:, k : k + 1]
+        silu_val, silu_slope = silu_terms(tot[:, :H])
+        up_pre, hid_grad = tot[:, H:H2], gate * tot[:, H2:]
+        AA[q, :, k * H3 : k * H3 + H] = (hid_grad * up_pre * silu_slope).astype(BF16)
+        AA[q, :, k * H3 + H : k * H3 + H2] = (hid_grad * silu_val).astype(BF16)
+        AA[q, :, k * H3 + H2 : (k + 1) * H3] = (gate * (silu_val * up_pre)).astype(BF16)
+    for j in range(1, E):
+        start(6, j, AA.at[q], AA.at[q])
+    for j in range(E):
+        if j:
+            got(6, j, AA)
+        p = peer(j)
+        ids = IDS[p].astype(F32)
+        rows = pl.ds(pl.multiple_of(p * T, T), T)
+        a0 = AA[p, :, :H3].astype(F32)
+        a1 = AA[p, :, H3:].astype(F32)
+        for e in range(E):
+            m0 = (ids[:, 0:1] == e).astype(F32)
+            m1 = (ids[:, 1:2] == e).astype(F32)
+            v = (m0 * a0 + m1 * a1).astype(BF16)
+            GU[rows, e * H2 : (e + 1) * H2] = v[:, :H2]
+            HD[rows, e * H : (e + 1) * H] = v[:, H2:]
+
+    def weight_rows(zz, cc):
+        s = 2 * zz + cc
+        pg = contract_rows(X[:, s].reshape(E * T, S), GU[...])
+        pd = contract_rows(Y[:, s].reshape(E * T, S), HD[...])
+        for e in range(E):
+            m = TM[e, pl.ds(s, 1), :]
+            DW[s, e, :, :H] = (pg[:, e * H2 : e * H2 + H] * m).astype(BF16)
+            DW[s, e, :, H:H2] = (pg[:, e * H2 + H : (e + 1) * H2] * m).astype(BF16)
+            DW[s, e, :, H2:] = (pd[:, e * H : (e + 1) * H] * m).astype(BF16)
+
+    def sib_copy(zz):
+        return rcopy(DW.at[2 * zz + 1 - c], SB.at[zz], bs.at[zz], br.at[zz], sib)
+
+    def up_copy(t):
+        return rcopy(DW.at[2 * t + c], UP.at[t], us.at[0, t], ur.at[0, t], above)
+
+    def dn_copy(t):
+        return rcopy(DW.at[2 * t + c], DN.at[t], us.at[1, t], ur.at[1, t], below)
+
+    order = []
+    for i in range((Z + 1) // 2):
+        order += [Z - 1 - i] + ([i] if i != Z - 1 - i else [])
+    for t in order:
+        weight_rows(t, 1 - c)
+        sib_copy(t).start()
+    for t in order:
+        weight_rows(t, c)
+
+    def send_grads(t):
+        s = 2 * t + c
+        sib_copy(t).wait_recv()
+
+        @pl.when(t > z)
+        def _():
+            @pl.when(has_dn)
+            def _():
+                up_copy(t).wait_recv()
+                DW[s] = (DW[s].astype(F32) + SB[t].astype(F32) + UP[t].astype(F32)).astype(BF16)
+
+            @pl.when(z == 0)
+            def _():
+                DW[s] = (DW[s].astype(F32) + SB[t].astype(F32)).astype(BF16)
+
+            up_copy(t).start()
+
+        @pl.when(t < z)
+        def _():
+            @pl.when(has_up)
+            def _():
+                dn_copy(t).wait_recv()
+                DW[s] = (DW[s].astype(F32) + SB[t].astype(F32) + DN[t].astype(F32)).astype(BF16)
+
+            @pl.when(z == Z - 1)
+            def _():
+                DW[s] = (DW[s].astype(F32) + SB[t].astype(F32)).astype(BF16)
+
+            dn_copy(t).start()
+
+    def input_rows(s):
+        tot = jnp.zeros((E * T, S), F32)
+        for e in range(E):
+            tot = tot + lax.dot_general(
+                GU[:, e * H2 : (e + 1) * H2],
+                W[s, e, :, :H2],
+                (((1,), (1,)), ((), ())),
+                preferred_element_type=F32,
+            )
+        DX[:, s] = tot.astype(BF16).reshape(E, T, S)
+
+    for i, t in enumerate(order):
+        send_grads(t)
+        if i == 1 or Z == 1:
+            def body(s, carry):
+                input_rows(s)
+                return carry
+
+            lax.fori_loop(0, R, body, 0)
+            for j in range(1, E):
+                start(7, j, DX.at[peer(j)], dx_out.at[q])
+            dx_out[q] = DX[q]
+
+    for e in range(E):
+        FS[e] = DW[r, e].astype(F32) + SB[z, e].astype(F32)
+
+    @pl.when(has_dn)
+    def _():
+        up_copy(z).wait_recv()
+        FS[...] += UP[z].astype(F32)
+
+    @pl.when(has_up)
+    def _():
+        dn_copy(z).wait_recv()
+        FS[...] += DN[z].astype(F32)
+
+    for e in range(E):
+        DW[r, e] = FS[e].astype(BF16)
+    for j in range(1, E):
+        start(8, j, DW.at[r, peer(j)], FW.at[q])
+    dw_out[q] = FS[q]
+    for j in range(1, E):
+        got(8, j, FW)
+        p = peer(j)
+        dw_out[p] = FW[p].astype(F32)
+    for j in range(1, E):
+        got(7, j, dx_out)
+
+    for d in sent:
+        d.wait_send()
+    for t in range(Z):
+        w_sib(t).wait_send()
+        sib_copy(t).wait_send()
+
+        @pl.when((t <= z) & has_up)
+        def _():
+            w_up(t).wait_send()
+
+        @pl.when((t >= z) & has_dn)
+        def _():
+            w_dn(t).wait_send()
+
+        @pl.when(t > z)
+        def _():
+            up_copy(t).wait_send()
+
+        @pl.when(t < z)
+        def _():
+            dn_copy(t).wait_send()
+
+
+def by_width(tokens, grad_out, gates, expert_ids, w_all, touched):
+    E, R = lax.axis_size("exp"), lax.axis_size("rep")
+    T, D = tokens.shape
+    S = D // (R * E)
+    H = w_all.shape[2] // 3
+    Z = R // 2
+
+    def cut(a):
+        return a.reshape(T, R, E, S).transpose(2, 1, 0, 3)
+
+    w = w_all[0].reshape(E, S, 3 * H)
+    ids = jnp.pad(expert_ids.astype(BF16), ((0, 0), (0, 128 - 2)))
+    tm = jnp.broadcast_to(
+        touched[0, 0].reshape(R, E).T.astype(F32)[:, :, None], (E, R, 128)
+    )
+    vm = pl.BlockSpec(memory_space=pltpu.VMEM)
+    dma = pltpu.SemaphoreType.DMA
+    dx, dw = pl.pallas_call(
+        functools.partial(kernel, R, E, T, S, H),
+        out_shape=(
+            jax.ShapeDtypeStruct((E, R, T, S), BF16),
+            jax.ShapeDtypeStruct((E, S, 3 * H), F32),
+        ),
+        in_specs=[vm] * 6,
+        out_specs=(vm, vm),
+        scratch_shapes=[
+            pltpu.VMEM((E, R, T, S), BF16),
+            pltpu.VMEM((E, R, T, S), BF16),
+            pltpu.VMEM((E, T, 128), BF16),
+            pltpu.VMEM((E, R, 128), F32),
+            pltpu.VMEM((R, E, S, 3 * H), BF16),
+            pltpu.VMEM((E * T, E * 3 * H), F32),
+            pltpu.VMEM((E, T, 6 * H), BF16),
+            pltpu.VMEM((E, T, 6 * H), BF16),
+            pltpu.VMEM((E, T, 6 * H), BF16),
+            pltpu.VMEM((E * T, E * 2 * H), BF16),
+            pltpu.VMEM((E * T, E * H), BF16),
+            pltpu.VMEM((E, R, T, S), BF16),
+            pltpu.VMEM((R, E, S, 3 * H), BF16),
+            pltpu.VMEM((Z, E, S, 3 * H), BF16),
+            pltpu.VMEM((Z, E, S, 3 * H), BF16),
+            pltpu.VMEM((Z, E, S, 3 * H), BF16),
+            pltpu.VMEM((E, S, 3 * H), F32),
+            pltpu.VMEM((E, S, 3 * H), BF16),
+            dma((9, E)),
+            dma((9, E)),
+            dma((R,)),
+            dma((3, Z)),
+            dma((Z,)),
+            dma((Z,)),
+            dma((2, Z)),
+            dma((2, Z)),
+            dma((1,)),
+        ],
+        compiler_params=pltpu.CompilerParams(
+            collective_id=0, has_side_effects=True, vmem_limit_bytes=52 * 1024 * 1024
+        ),
+    )(cut(tokens), cut(grad_out), w, ids, tm, gates)
+    token_grad = dx.transpose(2, 1, 0, 3).reshape(T, D)
+    return token_grad, dw.reshape(1, E * S, 3 * H)
+
+
+def by_expert(tokens, grad_out, gates, expert_ids, w_all, touched):
     tok_count = tokens.shape[0]
     model_width = tokens.shape[1]
     expert_count = lax.axis_size("exp")
@@ -80,7 +474,7 @@
     ).astype(jnp.float32)
     slot_grad = lax.dot_general(
         both_grad,
-        lax.all_gather(w_local[:, : 2 * hidden_count], "rep", axis=0, tiled=True),
+        shard_rows[:, : 2 * hidden_count],
         (((1,), (1,)), ((), ())),
         preferred_element_type=jnp.float32,
     )
@@ -95,6 +489,15 @@
     returned = returned.reshape(slot_count, model_width)
     token_grad = contract_rows(place_token, returned).astype(jnp.bfloat16)
     return (token_grad, owned[None])
+
+
+def per_device(tokens, grad_out, gates, expert_ids, w_all, touched):
+    R, E = lax.axis_size("rep"), lax.axis_size("exp")
+    share, rest = divmod(tokens.shape[1], R * E)
+    fits = rest == 0 and share == 128 and R % 16 in (0, 8)
+    fits = fits and tokens.shape[0] % 16 == 0 and w_all.shape[2] == 3 * 128
+    plan = by_width if fits else by_expert
+    return plan(tokens, grad_out, gates, expert_ids, w_all, touched)
 
 
 def solution(mesh):

time: 147 us -> 141 us (0.959)
  the two profiles are of different devices: /device:TPU:0 before, /device:TPU:8 now
where the time goes in v1:
time: 141 us
  Pallas kernels  129 us (91%)
  local copies, waits for them, and re-layouts  11.2 us (8%)
    pallas_call x1, Pallas kernels, by_width(): pl.pallas_call(functools.partial(kernel, R, E, T, S, H), out_shape=(jax.S...  129 us
    unnamed x15, local copies, waits for them, and re-layouts  6.56 us

profile of v1, /device:TPU:8, one launch (start us, length us, event | category | flops | bytes accessed | tf_op | source)
XLA Modules:
  0.0 140.8 jit_solution(5028028199630507762)
XLA Ops:
  0.6 0.0 copy-start.3
  0.6 0.7 copy-done.3
  1.3 0.0 copy-start.4
  1.3 0.6 copy-done.4
  2.0 0.1 convert_element_type.16
  2.1 0.1 copy.25
  2.2 0.1 broadcast_in_dim.2.tm_ref
  2.2 0.1 copy.24
  2.4 0.0 copy-start.2
  2.4 0.7 copy-done.2
  3.0 0.1 copy.26.gate_ref
  3.2 1.6 %copy.20 = bf16[128,4096]{0,1:T(8,128)(2,1)S(1)} copy(bf16[128,4096]{1,0:T(8,128)(2,1)} %param.6) | data formatting | bytes 2097152 | tf_op args[0]
  4.8 0.0 copy-start.1
  4.8 1.3 copy.21
  6.1 0.0 copy-done.1
  6.1 0.7 copy.22
  6.8 0.0 copy-start
  6.8 1.3 copy.23
  8.1 0.0 copy-done
  8.1 128.9 %shard_map.77 = (bf16[4,8,128,128]{3,2,1,0:T(8,128)(2,1)}, f32[4,128,384]{2,1,0:T(8,128)S(1)}) custom-call(bf16[4,8,128,128]{3,2,1,0:T(8,128)(2,1)} %bitcast.11, bf16[4,8,128,128]{3,2,1,0:T(8,128)(2,1)} %bitcast.12, bf16[4,128,384]{2,1,0:T(8,128)(2,1)S(1)} %bitcast.10, bf16[128,128]{1,0:T(8,128)(2,1)S(1)} %pad.4.id_ref, ...), custom_call_target="tpu_custom_call" | custom-call | tf_op jit(solution)/shard_map/pallas_call | solution.py:367
  137.0 1.6 %copy.27 = bf16[128,8,4,128]{0,3,2,1:T(8,128)(2,1)S(1)} copy(bf16[128,8,4,128]{3,0,1,2:T(8,128)(2,1)} %bitcast.16) | data formatting | bytes 2097152 | tf_op jit(solution)/shard_map/transpose | solution.py:408
  138.6 1.3 copy.28
  139.9 0.9 copy.30
  (3 shorter events, 0.0 us)
Async XLA Ops:
  0.6 0.7 copy-start.3
  1.3 0.7 copy-start.4
  2.4 0.7 copy-start.2
  4.8 1.3 copy-start.1
  6.8 1.3 copy-start

commit v2 on v0

--- a/solution.py
+++ b/solution.py
@@ -1,7 +1,14 @@
+import functools
 import jax
 import jax.numpy as jnp
 from jax import lax
+from jax.experimental import pallas as pl
+from jax.experimental.pallas import tpu as pltpu
 from jax.sharding import PartitionSpec as P
+
+MESH = pl.DeviceIdType.MESH
+BF16 = jnp.bfloat16
+F32 = jnp.float32
 
 
 def silu_terms(gate_pre):
@@ -15,7 +22,486 @@
     )
 
 
-def per_device(tokens, grad_out, gates, expert_ids, w_all, touched):
+def kernel(
+    R, E, T, S, H,
+    x_ref, g_ref, w_ref, id_ref, tm_ref, gate_ref,
+    dx_out, dw_out,
+    X, Y, IDS, TM, WG, WD, CG, CD, PG, PD, QG, QD, AG, AD, GU, HD, DX,
+    DG, DD, BG, BD, UG, UD, NG, ND, FG, FD, RG, RD,
+    a2s, a2r, wr, ws, bs, br, us, ur, loc,
+):
+    H2 = 2 * H
+    Z = R // 2
+    r = lax.axis_index("rep")
+    q = lax.axis_index("exp")
+    z, c = r // 2, lax.rem(r, 2)
+    sib = (2 * z + 1 - c, q)
+    above = (lax.rem(r + 2, R), q)
+    below = (lax.rem(r + R - 2, R), q)
+    has_up, has_dn = z < Z - 1, z > 0
+
+    def peer(j):
+        return lax.rem(q + j, E)
+
+    def span(s, p):
+        return pl.ds(pl.multiple_of((s * E + p) * S, S), S)
+
+    def own_cols(s, carry):
+        pltpu.make_async_copy(x_ref.at[:, span(s, q)], X.at[q, s], loc.at[0]).start()
+        pltpu.make_async_copy(g_ref.at[:, span(s, q)], Y.at[q, s], loc.at[1]).start()
+        return carry
+
+    lax.fori_loop(0, R, own_cols, 0)
+
+    barrier = pltpu.get_barrier_semaphore()
+    for j in range(1, E):
+        pl.semaphore_signal(barrier, inc=1, device_id=(r, peer(j)), device_id_type=MESH)
+    pl.semaphore_signal(barrier, inc=1, device_id=sib, device_id_type=MESH)
+
+    @pl.when(has_up)
+    def _():
+        pl.semaphore_signal(barrier, inc=1, device_id=above, device_id_type=MESH)
+
+    @pl.when(has_dn)
+    def _():
+        pl.semaphore_signal(barrier, inc=1, device_id=below, device_id_type=MESH)
+
+    edge = jnp.where(z == 0, 1, 0) + jnp.where(z == Z - 1, 1, 0)
+    pl.semaphore_wait(barrier, E + 2 - edge)
+
+    def rcopy(src, dst, ss, rs, dev):
+        return pltpu.make_async_remote_copy(
+            src_ref=src, dst_ref=dst, send_sem=ss, recv_sem=rs, device_id=dev, device_id_type=MESH
+        )
+
+    sent = []
+
+    def copy_to(kind, j, src, dst):
+        return rcopy(src, dst, a2s.at[kind, j], a2r.at[kind, q], (r, peer(j)))
+
+    def start(kind, j, src, dst):
+        d = copy_to(kind, j, src, dst)
+        d.start()
+        sent.append(d)
+
+    def got(kind, j, dst):
+        p = peer(j)
+        rcopy(dst, dst, a2s.at[kind, j], a2r.at[kind, p], (r, p)).wait_recv()
+
+    for j in range(1, E):
+        start(0, j, w_ref.at[peer(j), :, :H2], WG.at[r, q])
+    for j in range(1, E):
+        start(1, j, w_ref.at[peer(j), :, H2:], WD.at[r, q])
+    for j in range(1, E):
+        start(2, j, id_ref, IDS.at[q])
+        start(3, j, tm_ref.at[peer(j)], TM.at[q])
+
+    def send_cols(kind, src, buf):
+        def body(s, carry):
+            for j in range(1, E):
+                copy_to(kind, j, src.at[:, span(s, peer(j))], buf.at[q, s]).start()
+            return carry
+
+        lax.fori_loop(0, R, body, 0)
+        for j in range(1, E):
+            sent.append(copy_to(kind, j, buf.at[q], buf.at[q]))
+
+    send_cols(4, x_ref, X)
+    send_cols(5, g_ref, Y)
+    WG[r, q] = w_ref[q, :, :H2]
+    WD[r, q] = w_ref[q, :, H2:]
+    IDS[q] = id_ref[...]
+    TM[q] = tm_ref[q]
+
+    WP = (WG, WD)
+
+    def w_copy(p, way, zz):
+        s = 2 * zz + c
+        dev = (above, below, sib)[way]
+        return rcopy(WP[p].at[s], WP[p].at[s], ws.at[p, way, zz], wr.at[p, s], dev)
+
+    def w_wait(p, s):
+        rcopy(WP[p].at[s], WP[p].at[s], ws.at[p, 2, 0], wr.at[p, s], sib).wait_recv()
+
+    def w_first(p):
+        for j in range(1, E):
+            got(p, j, WP[p].at[r, peer(j)])
+
+        @pl.when(has_up)
+        def _():
+            w_copy(p, 0, z).start()
+
+        @pl.when(has_dn)
+        def _():
+            w_copy(p, 1, z).start()
+
+        w_copy(p, 2, z).start()
+
+    def w_forward(p, d):
+        lo, hi = z - d, z + d
+
+        @pl.when(lo >= 0)
+        def _():
+            w_wait(p, 2 * lo + c)
+
+            @pl.when(has_up)
+            def _():
+                w_copy(p, 0, lo).start()
+
+            w_copy(p, 2, lo).start()
+
+        @pl.when(hi < Z)
+        def _():
+            w_wait(p, 2 * hi + c)
+
+            @pl.when(has_dn)
+            def _():
+                w_copy(p, 1, hi).start()
+
+            w_copy(p, 2, hi).start()
+
+    def project(p, s, first=False):
+        src, wid, acc = ((X, H2, CG), (Y, H, CD))[p]
+        rows = src[:, s].reshape(E * T, S)
+        for e in range(E):
+            v = jnp.dot(rows, WP[p][s, e], preferred_element_type=F32)
+            if first:
+                acc[:, e * wid : (e + 1) * wid] = v
+            else:
+                acc[:, e * wid : (e + 1) * wid] += v
+
+    def project_at(p, d):
+        if d == 0:
+            project(p, r, True)
+            w_wait(p, 2 * z + 1 - c)
+            project(p, 2 * z + 1 - c)
+            return
+        for zz, there in ((z - d, z - d >= 0), (z + d, z + d < Z)):
+
+            @pl.when(there)
+            def _():
+                project(p, 2 * zz + c)
+                w_wait(p, 2 * zz + 1 - c)
+                project(p, 2 * zz + 1 - c)
+
+    w_first(0)
+    w_first(1)
+    for j in range(1, E):
+        got(2, j, IDS.at[peer(j)])
+        got(3, j, TM.at[peer(j)])
+    if Z > 1:
+        w_forward(0, 1)
+        w_forward(1, 1)
+    pltpu.make_async_copy(X.at[q], X.at[q], loc.at[0]).wait()
+    for j in range(1, E):
+        got(4, j, X.at[peer(j)])
+    project_at(0, 0)
+    if Z > 2:
+        w_forward(0, 2)
+    if Z > 1:
+        project_at(0, 1)
+    pltpu.make_async_copy(Y.at[q], Y.at[q], loc.at[1]).wait()
+    for j in range(1, E):
+        got(5, j, Y.at[peer(j)])
+    if Z > 2:
+        w_forward(1, 2)
+    project_at(1, 0)
+    if Z > 1:
+        project_at(1, 1)
+    for d in range(3, Z):
+        w_forward(0, d)
+        project_at(0, d - 1)
+        if d < Z - 1:
+            w_forward(1, d)
+            project_at(1, d - 1)
+    if Z > 2:
+        project_at(0, Z - 1)
+
+    def pairs(p):
+        wid, acc, buf, dst = ((H2, CG, PG, QG), (H, CD, PD, QD))[p]
+        for j in list(range(1, E)) + [0]:
+            o = peer(j)
+            ids = IDS[o].astype(F32)
+            rows = pl.ds(pl.multiple_of(o * T, T), T)
+            for k in range(2):
+                tot = jnp.zeros((T, wid), F32)
+                for e in range(E):
+                    m = (ids[:, k : k + 1] == e).astype(F32)
+                    tot = tot + m * acc[rows, e * wid : (e + 1) * wid]
+                buf[o, :, k * wid : (k + 1) * wid] = tot.astype(BF16)
+            if j:
+                start(6 + p, j, buf.at[o], dst.at[q])
+
+    def pair_sum(p, k):
+        wid, buf, dst = ((H2, PG, QG), (H, PD, QD))[p]
+        tot = buf[q, :, k * wid : (k + 1) * wid].astype(F32)
+        for j in range(1, E):
+            tot = tot + dst[peer(j), :, k * wid : (k + 1) * wid].astype(F32)
+        return tot
+
+    pairs(0)
+    if Z > 3:
+        w_forward(1, Z - 1)
+        project_at(1, Z - 2)
+    if Z > 2:
+        project_at(1, Z - 1)
+    pairs(1)
+    for j in range(1, E):
+        got(6, j, QG.at[peer(j)])
+    acts = []
+    for k in range(2):
+        tot = pair_sum(0, k)
+        silu_val, silu_slope = silu_terms(tot[:, :H])
+        up_pre, gate = tot[:, H:], gate_ref[:, k : k + 1]
+        acts.append((gate * up_pre * silu_slope, gate * silu_val))
+        AD[q, :, k * H : (k + 1) * H] = (gate * (silu_val * up_pre)).astype(BF16)
+    for j in range(1, E):
+        start(8, j, AD.at[q], AD.at[q])
+    for j in range(1, E):
+        got(7, j, QD.at[peer(j)])
+    for k in range(2):
+        hid_grad = pair_sum(1, k)
+        AG[q, :, k * H2 : k * H2 + H] = (hid_grad * acts[k][0]).astype(BF16)
+        AG[q, :, k * H2 + H : (k + 1) * H2] = (hid_grad * acts[k][1]).astype(BF16)
+    for j in range(1, E):
+        start(9, j, AG.at[q], AG.at[q])
+
+    def spread(p):
+        wid, src, dst = ((H2, AG, GU), (H, AD, HD))[p]
+        for j in range(E):
+            o = peer(j)
+            if j:
+                got(9 - p, j, src.at[o])
+            ids = IDS[o].astype(F32)
+            rows = pl.ds(pl.multiple_of(o * T, T), T)
+            a0 = src[o, :, :wid].astype(F32)
+            a1 = src[o, :, wid:].astype(F32)
+            for e in range(E):
+                m0 = (ids[:, 0:1] == e).astype(F32)
+                m1 = (ids[:, 1:2] == e).astype(F32)
+                dst[rows, e * wid : (e + 1) * wid] = (m0 * a0 + m1 * a1).astype(BF16)
+
+    DP, BP, UP, NP = (DG, DD), (BG, BD), (UG, UD), (NG, ND)
+
+    def weight_rows(p, s):
+        src, wid, act = ((X, H2, GU), (Y, H, HD))[p]
+        v = contract_rows(src[:, s].reshape(E * T, S), act[...])
+        for e in range(E):
+            m = TM[e, pl.ds(s, 1), :]
+            for h in range(0, wid, H):
+                DP[p][s, e, :, h : h + H] = (v[:, e * wid + h : e * wid + h + H] * m).astype(BF16)
+
+    def sib_copy(p, t):
+        return rcopy(DP[p].at[2 * t + 1 - c], BP[p].at[t], bs.at[p, t], br.at[p, t], sib)
+
+    def up_copy(p, t):
+        return rcopy(DP[p].at[2 * t + c], UP[p].at[t], us.at[p, 0, t], ur.at[p, 0, t], above)
+
+    def dn_copy(p, t):
+        return rcopy(DP[p].at[2 * t + c], NP[p].at[t], us.at[p, 1, t], ur.at[p, 1, t], below)
+
+    def grads(p, i):
+        t = jnp.where(z < (Z + 1) // 2, Z - 1 - i, i)
+        weight_rows(p, 2 * t + 1 - c)
+        sib_copy(p, t).start()
+        weight_rows(p, 2 * t + c)
+
+    def add_in(p, t, others):
+        s = 2 * t + c
+        for e in range(E):
+            tot = DP[p][s, e].astype(F32)
+            for o in others:
+                tot = tot + o[t, e].astype(F32)
+            DP[p][s, e] = tot.astype(BF16)
+
+    def chain(p, n):
+        @pl.when(n >= z)
+        def _():
+            t = Z - 1 + z - n
+            sib_copy(p, t).wait_recv()
+
+            @pl.when(has_dn)
+            def _():
+                up_copy(p, t).wait_recv()
+                add_in(p, t, (BP[p], UP[p]))
+
+            @pl.when(z == 0)
+            def _():
+                add_in(p, t, (BP[p],))
+
+            up_copy(p, t).start()
+
+        @pl.when(n >= Z - 1 - z)
+        def _():
+            t = n - (Z - 1 - z)
+            sib_copy(p, t).wait_recv()
+
+            @pl.when(has_up)
+            def _():
+                dn_copy(p, t).wait_recv()
+                add_in(p, t, (BP[p], NP[p]))
+
+            @pl.when(z == Z - 1)
+            def _():
+                add_in(p, t, (BP[p],))
+
+            dn_copy(p, t).start()
+
+    def finish(p):
+        fs, fin = ((FG, RG), (FD, RD))[p]
+        sib_copy(p, z).wait_recv()
+        for e in range(E):
+            fs[e] = DP[p][r, e].astype(F32) + BP[p][z, e].astype(F32)
+
+        @pl.when(has_dn)
+        def _():
+            up_copy(p, z).wait_recv()
+            fs[...] += UP[p][z].astype(F32)
+
+        @pl.when(has_up)
+        def _():
+            dn_copy(p, z).wait_recv()
+            fs[...] += NP[p][z].astype(F32)
+
+        for e in range(E):
+            DP[p][r, e] = fs[e].astype(BF16)
+        for j in range(1, E):
+            start(12 - p, j, DP[p].at[r, peer(j)], fin.at[q])
+
+    def place(p):
+        cols, fs, fin = ((slice(0, H2), FG, RG), (slice(H2, 3 * H), FD, RD))[p]
+        dw_out[q, :, cols] = fs[q]
+        for j in range(1, E):
+            got(12 - p, j, fin.at[peer(j)])
+            dw_out[peer(j), :, cols] = fin[peer(j)].astype(F32)
+
+    def input_rows(s, carry):
+        tot = jnp.zeros((E * T, S), F32)
+        for e in range(E):
+            tot = tot + lax.dot_general(
+                GU[:, e * H2 : (e + 1) * H2],
+                WG[s, e],
+                (((1,), (1,)), ((), ())),
+                preferred_element_type=F32,
+            )
+        DX[:, s] = tot.astype(BF16).reshape(E, T, S)
+        for j in range(1, E):
+            copy_to(10, j, DX.at[peer(j), s], dx_out.at[:, span(s, q)]).start()
+        dx_out[:, span(s, q)] = DX[q, s]
+        return carry
+
+    spread(1)
+    for i in range(Z):
+        grads(1, i)
+    if Z > 1:
+        chain(1, 0)
+    spread(0)
+    for i in range(Z):
+        grads(0, i)
+        if i == min(1, Z - 1) and Z > 2:
+            chain(1, 1)
+    if Z > 1:
+        chain(0, 0)
+    for n in range(2, Z - 1):
+        chain(1, n)
+        if n < Z - 2:
+            chain(0, n - 1)
+    lax.fori_loop(0, R, input_rows, 0)
+    for j in range(1, E):
+        sent.append(copy_to(10, j, DX.at[q], DX.at[q]))
+    for n in range(max(1, Z - 3), Z - 1):
+        chain(0, n)
+    finish(1)
+    finish(0)
+    place(1)
+    place(0)
+    for j in range(1, E):
+        got(10, j, DX.at[peer(j)])
+
+    for d in sent:
+        d.wait_send()
+    for p in range(2):
+        for t in range(Z):
+            w_copy(p, 2, t).wait_send()
+            sib_copy(p, t).wait_send()
+
+            @pl.when((t <= z) & has_up)
+            def _():
+                w_copy(p, 0, t).wait_send()
+
+            @pl.when((t >= z) & has_dn)
+            def _():
+                w_copy(p, 1, t).wait_send()
+
+            @pl.when(t > z)
+            def _():
+                up_copy(p, t).wait_send()
+
+            @pl.when(t < z)
+            def _():
+                dn_copy(p, t).wait_send()
+
+
+def by_width(tokens, grad_out, gates, expert_ids, w_all, touched):
+    E, R = lax.axis_size("exp"), lax.axis_size("rep")
+    T, D = tokens.shape
+    S = D // (R * E)
+    H = w_all.shape[2] // 3
+    Z = R // 2
+    w = w_all[0].reshape(E, S, 3 * H)
+    ids = jnp.pad(expert_ids.astype(BF16), ((0, 0), (0, 128 - 2)))
+    tm = jnp.broadcast_to(
+        touched[0, 0].reshape(R, E).T.astype(F32)[:, :, None], (E, R, 128)
+    )
+    vm = pl.BlockSpec(memory_space=pltpu.VMEM)
+    hbm = pl.BlockSpec(memory_space=pl.ANY)
+    dma = pltpu.SemaphoreType.DMA
+
+    def two(*lead, kind=BF16, times=1):
+        return [pltpu.VMEM(lead + (times * 2 * H,), kind), pltpu.VMEM(lead + (times * H,), kind)]
+
+    wide = pltpu.VMEM((E, R, T, S), BF16)
+    dx, dw = pl.pallas_call(
+        functools.partial(kernel, R, E, T, S, H),
+        out_shape=(
+            jax.ShapeDtypeStruct((T, D), BF16),
+            jax.ShapeDtypeStruct((E, S, 3 * H), F32),
+        ),
+        in_specs=[hbm] * 2 + [vm] * 4,
+        out_specs=(vm, vm),
+        scratch_shapes=[wide, wide, pltpu.VMEM((E, T, 128), BF16), pltpu.VMEM((E, R, 128), F32)]
+        + two(R, E, S)
+        + two(E * T, kind=F32, times=E)
+        + two(E, T, times=2)
+        + two(E, T, times=2)
+        + two(E, T, times=2)
+        + two(E * T, times=E)
+        + [wide]
+        + two(R, E, S)
+        + two(Z, E, S)
+        + two(Z, E, S)
+        + two(Z, E, S)
+        + two(E, S, kind=F32)
+        + two(E, S)
+        + [
+            dma((13, E)),
+            dma((13, E)),
+            dma((2, R)),
+            dma((2, 3, Z)),
+            dma((2, Z)),
+            dma((2, Z)),
+            dma((2, 2, Z)),
+            dma((2, 2, Z)),
+            dma((2,)),
+        ],
+        compiler_params=pltpu.CompilerParams(
+            collective_id=0, has_side_effects=True, vmem_limit_bytes=52 * 1024 * 1024
+        ),
+    )(tokens, grad_out, w, ids, tm, gates)
+    return dx, dw.reshape(1, E * S, 3 * H)
+
+
+def by_expert(tokens, grad_out, gates, expert_ids, w_all, touched):
     tok_count = tokens.shape[0]
     model_width = tokens.shape[1]
     expert_count = lax.axis_size("exp")
@@ -80,7 +566,7 @@
     ).astype(jnp.float32)
     slot_grad = lax.dot_general(
         both_grad,
-        lax.all_gather(w_local[:, : 2 * hidden_count], "rep", axis=0, tiled=True),
+        shard_rows[:, : 2 * hidden_count],
         (((1,), (1,)), ((), ())),
         preferred_element_type=jnp.float32,
     )
@@ -95,6 +581,15 @@
     returned = returned.reshape(slot_count, model_width)
     token_grad = contract_rows(place_token, returned).astype(jnp.bfloat16)
     return (token_grad, owned[None])
+
+
+def per_device(tokens, grad_out, gates, expert_ids, w_all, touched):
+    R, E = lax.axis_size("rep"), lax.axis_size("exp")
+    share, rest = divmod(tokens.shape[1], R * E)
+    fits = rest == 0 and share == 128 and R % 16 in (0, 8)
+    fits = fits and tokens.shape[0] % 16 == 0 and w_all.shape[2] == 3 * 128
+    plan = by_width if fits else by_expert
+    return plan(tokens, grad_out, gates, expert_ids, w_all, touched)
 
 
 def solution(mesh):

time: 147 us -> 97.8 us (0.67)
  the two profiles are of different devices: /device:TPU:0 before, /device:TPU:8 now
where the time goes in v2:
time: 97.8 us; the launch traced here: 96.4 us
  Pallas kernels  89.1 us (91%)
  local copies, waits for them, and re-layouts  6.64 us (7%)
    pallas_call x1, Pallas kernels, by_width(): pl.pallas_call(functools.partial(kernel, R, E, T, S, H), out_shape=(jax.S...  89.1 us
    unnamed x11, local copies, waits for them, and re-layouts  6.25 us

profile of v2, /device:TPU:8, one launch (start us, length us, event | category | flops | bytes accessed | tf_op | source)
XLA Modules:
  0.0 96.4 jit_solution(11574968398705641652)
XLA Ops:
  0.6 0.0 copy-start.2
  0.6 0.7 copy-done.2
  1.3 0.0 copy-start.3
  1.3 0.6 copy-done.3
  2.0 0.1 convert_element_type.16
  2.1 0.1 copy.15
  2.2 0.1 broadcast_in_dim.2.tm_ref
  2.2 0.1 copy.14
  2.4 0.0 copy-start.1
  2.4 0.7 copy-done.1
  3.0 0.1 copy.16.gate_ref
  3.2 0.0 copy-start
  3.2 1.0 %copy-done = bf16[1,512,384]{2,1,0:T(8,128)(2,1)S(1)} copy-done((bf16[1,512,384]{2,1,0:T(8,128)(2,1)S(1)}, bf16[1,512,384]{2,1,0:T(8,128)(2,1)}, u32[]{:S(2)}) %copy-start) | copy-done | bytes 393240
  4.2 89.1 %shard_map.77 = (bf16[128,4096]{1,0:T(8,128)(2,1)}, f32[4,128,384]{2,1,0:T(8,128)S(1)}) custom-call(bf16[128,4096]{1,0:T(8,128)(2,1)} %x_ref.1, bf16[128,4096]{1,0:T(8,128)(2,1)} %g_ref.1, bf16[4,128,384]{2,1,0:T(8,128)(2,1)S(1)} %bitcast.4, bf16[128,128]{1,0:T(8,128)(2,1)S(1)} %pad.4.id_ref, f32[4,8,128]{2,1,0:T(8,128)S(1)} %broadcast_in_dim.2.tm_ref, ...), custom_call_target="tpu_custom_call" | custom-call | tf_op jit(solution)/shard_map/pallas_call | solution.py:464
  93.3 2.3 %copy.19 = bf16[128,4096]{1,0:T(8,128)(2,1)} copy(bf16[128,4096]{1,0:T(8,128)(2,1)} %get-tuple-element.8) | data formatting | bytes 2097152
  95.6 0.9 copy.20
  (3 shorter events, 0.0 us)
Async XLA Ops:
  0.6 0.7 copy-start.2
  1.3 0.7 copy-start.3
  2.4 0.7 copy-start.1
  3.2 1.0 %copy-start = (bf16[1,512,384]{2,1,0:T(8,128)(2,1)S(1)}, bf16[1,512,384]{2,1,0:T(8,128)(2,1)}, u32[]{:S(2)}) copy-start(bf16[1,512,384]{2,1,0:T(8,128)(2,1)} %param.10) | copy-start | bytes 1179652

commit v3 on v2

--- a/solution.py
+++ b/solution.py
@@ -51,6 +51,8 @@
         pltpu.make_async_copy(g_ref.at[:, span(s, q)], Y.at[q, s], loc.at[1]).start()
         return carry
 
+    pltpu.make_async_copy(w_ref.at[q, :, :H2], WG.at[r, q], loc.at[2]).start()
+    pltpu.make_async_copy(w_ref.at[q, :, H2:], WD.at[r, q], loc.at[3]).start()
     lax.fori_loop(0, R, own_cols, 0)
 
     barrier = pltpu.get_barrier_semaphore()
@@ -88,10 +90,83 @@
         p = peer(j)
         rcopy(dst, dst, a2s.at[kind, j], a2r.at[kind, p], (r, p)).wait_recv()
 
+    WP = (WG, WD)
+
+    def w_copy(p, way, zz, e):
+        s = 2 * zz + c
+        dev = (above, below, sib)[way]
+        ref = WP[p].at[s, e]
+        return rcopy(ref, ref, ws.at[p, way, zz, e], wr.at[p, s, e], dev)
+
+    def w_wait(p, s, e):
+        ref = WP[p].at[s, e]
+        rcopy(ref, ref, ws.at[p, 2, 0, e], wr.at[p, s, e], sib).wait_recv()
+
+    def w_slot(p, s):
+        for j in range(E):
+            w_wait(p, s, peer(j))
+
+    def w_send(p, e):
+        @pl.when(has_up)
+        def _():
+            w_copy(p, 0, z, e).start()
+
+        @pl.when(has_dn)
+        def _():
+            w_copy(p, 1, z, e).start()
+
+        w_copy(p, 2, z, e).start()
+
+    def w_own(p):
+        w_send(p, q)
+
+    def w_first(p):
+        for j in range(1, E):
+            got(p, j, WP[p].at[r, peer(j)])
+            w_send(p, peer(j))
+
+    def w_forward(p, d):
+        lo, hi = z - d, z + d
+
+        def body(j, carry):
+            e = lax.rem(q + j, E)
+
+            @pl.when(lo >= 0)
+            def _():
+                w_wait(p, 2 * lo + c, e)
+
+                @pl.when(has_up)
+                def _():
+                    w_copy(p, 0, lo, e).start()
+
+                w_copy(p, 2, lo, e).start()
+
+            @pl.when(hi < Z)
+            def _():
+                w_wait(p, 2 * hi + c, e)
+
+                @pl.when(has_dn)
+                def _():
+                    w_copy(p, 1, hi, e).start()
+
+                w_copy(p, 2, hi, e).start()
+
+            return carry
+
+        lax.fori_loop(0, E, body, 0)
+
     for j in range(1, E):
         start(0, j, w_ref.at[peer(j), :, :H2], WG.at[r, q])
+    own_w = (
+        pltpu.make_async_copy(w_ref.at[q, :, :H2], WG.at[r, q], loc.at[2]),
+        pltpu.make_async_copy(w_ref.at[q, :, H2:], WD.at[r, q], loc.at[3]),
+    )
+    own_w[0].wait()
+    w_own(0)
     for j in range(1, E):
         start(1, j, w_ref.at[peer(j), :, H2:], WD.at[r, q])
+    own_w[1].wait()
+    w_own(1)
     for j in range(1, E):
         start(2, j, id_ref, IDS.at[q])
         start(3, j, tm_ref.at[peer(j)], TM.at[q])
@@ -108,57 +183,8 @@
 
     send_cols(4, x_ref, X)
     send_cols(5, g_ref, Y)
-    WG[r, q] = w_ref[q, :, :H2]
-    WD[r, q] = w_ref[q, :, H2:]
     IDS[q] = id_ref[...]
     TM[q] = tm_ref[q]
-
-    WP = (WG, WD)
-
-    def w_copy(p, way, zz):
-        s = 2 * zz + c
-        dev = (above, below, sib)[way]
-        return rcopy(WP[p].at[s], WP[p].at[s], ws.at[p, way, zz], wr.at[p, s], dev)
-
-    def w_wait(p, s):
-        rcopy(WP[p].at[s], WP[p].at[s], ws.at[p, 2, 0], wr.at[p, s], sib).wait_recv()
-
-    def w_first(p):
-        for j in range(1, E):
-            got(p, j, WP[p].at[r, peer(j)])
-
-        @pl.when(has_up)
-        def _():
-            w_copy(p, 0, z).start()
-
-        @pl.when(has_dn)
-        def _():
-            w_copy(p, 1, z).start()
-
-        w_copy(p, 2, z).start()
-
-    def w_forward(p, d):
-        lo, hi = z - d, z + d
-
-        @pl.when(lo >= 0)
-        def _():
-            w_wait(p, 2 * lo + c)
-
-            @pl.when(has_up)
-            def _():
-                w_copy(p, 0, lo).start()
-
-            w_copy(p, 2, lo).start()
-
-        @pl.when(hi < Z)
-        def _():
-            w_wait(p, 2 * hi + c)
-
-            @pl.when(has_dn)
-            def _():
-                w_copy(p, 1, hi).start()
-
-            w_copy(p, 2, hi).start()
 
     def project(p, s, first=False):
         src, wid, acc = ((X, H2, CG), (Y, H, CD))[p]
@@ -173,7 +199,7 @@
     def project_at(p, d):
         if d == 0:
             project(p, r, True)
-            w_wait(p, 2 * z + 1 - c)
+            w_slot(p, 2 * z + 1 - c)
             project(p, 2 * z + 1 - c)
             return
         for zz, there in ((z - d, z - d >= 0), (z + d, z + d < Z)):
@@ -181,7 +207,7 @@
             @pl.when(there)
             def _():
                 project(p, 2 * zz + c)
-                w_wait(p, 2 * zz + 1 - c)
+                w_slot(p, 2 * zz + 1 - c)
                 project(p, 2 * zz + 1 - c)
 
     w_first(0)
@@ -196,25 +222,12 @@
     for j in range(1, E):
         got(4, j, X.at[peer(j)])
     project_at(0, 0)
-    if Z > 2:
-        w_forward(0, 2)
-    if Z > 1:
-        project_at(0, 1)
-    pltpu.make_async_copy(Y.at[q], Y.at[q], loc.at[1]).wait()
-    for j in range(1, E):
-        got(5, j, Y.at[peer(j)])
-    if Z > 2:
-        w_forward(1, 2)
-    project_at(1, 0)
-    if Z > 1:
-        project_at(1, 1)
-    for d in range(3, Z):
+    for d in range(2, Z):
         w_forward(0, d)
         project_at(0, d - 1)
         if d < Z - 1:
             w_forward(1, d)
-            project_at(1, d - 1)
-    if Z > 2:
+    if Z > 1:
         project_at(0, Z - 1)
 
     def pairs(p):
@@ -240,11 +253,14 @@
         return tot
 
     pairs(0)
-    if Z > 3:
+    pltpu.make_async_copy(Y.at[q], Y.at[q], loc.at[1]).wait()
+    for j in range(1, E):
+        got(5, j, Y.at[peer(j)])
+    for d in range(Z - 1):
+        project_at(1, d)
+    if Z > 2:
         w_forward(1, Z - 1)
-        project_at(1, Z - 2)
-    if Z > 2:
-        project_at(1, Z - 1)
+    project_at(1, Z - 1)
     pairs(1)
     for j in range(1, E):
         got(6, j, QG.at[peer(j)])
@@ -294,11 +310,13 @@
     def sib_copy(p, t):
         return rcopy(DP[p].at[2 * t + 1 - c], BP[p].at[t], bs.at[p, t], br.at[p, t], sib)
 
-    def up_copy(p, t):
-        return rcopy(DP[p].at[2 * t + c], UP[p].at[t], us.at[p, 0, t], ur.at[p, 0, t], above)
-
-    def dn_copy(p, t):
-        return rcopy(DP[p].at[2 * t + c], NP[p].at[t], us.at[p, 1, t], ur.at[p, 1, t], below)
+    def up_copy(p, t, e):
+        src = DP[p].at[2 * t + c, e]
+        return rcopy(src, UP[p].at[t, e], us.at[p, 0, t, e], ur.at[p, 0, t, e], above)
+
+    def dn_copy(p, t, e):
+        src = DP[p].at[2 * t + c, e]
+        return rcopy(src, NP[p].at[t, e], us.at[p, 1, t, e], ur.at[p, 1, t, e], below)
 
     def grads(p, i):
         t = jnp.where(z < (Z + 1) // 2, Z - 1 - i, i)
@@ -306,67 +324,73 @@
         sib_copy(p, t).start()
         weight_rows(p, 2 * t + c)
 
-    def add_in(p, t, others):
-        s = 2 * t + c
-        for e in range(E):
-            tot = DP[p][s, e].astype(F32)
-            for o in others:
-                tot = tot + o[t, e].astype(F32)
-            DP[p][s, e] = tot.astype(BF16)
+    def add_in(p, t, e, others):
+        tot = DP[p][2 * t + c, e].astype(F32)
+        for o in others:
+            tot = tot + o[t, e].astype(F32)
+        DP[p][2 * t + c, e] = tot.astype(BF16)
+
+    def chain_ends(p, n):
+        def send(t, copy):
+            sib_copy(p, t).wait_recv()
+
+            def body(j, carry):
+                e = lax.rem(q + j, E)
+                add_in(p, t, e, (BP[p],))
+                copy(p, t, e).start()
+                return carry
+
+            lax.fori_loop(1, E + 1, body, 0)
+
+        @pl.when(z == 0)
+        def _():
+            send(Z - 1 - n, up_copy)
+
+        @pl.when(z == Z - 1)
+        def _():
+            send(n, dn_copy)
 
     def chain(p, n):
-        @pl.when(n >= z)
+        def send(t, copy, got_ref):
+            sib_copy(p, t).wait_recv()
+
+            def body(j, carry):
+                e = lax.rem(q + j, E)
+                copy(p, t, e).wait_recv()
+                add_in(p, t, e, (BP[p], got_ref))
+                copy(p, t, e).start()
+                return carry
+
+            lax.fori_loop(1, E + 1, body, 0)
+
+        @pl.when((n >= z) & has_dn)
         def _():
-            t = Z - 1 + z - n
-            sib_copy(p, t).wait_recv()
-
-            @pl.when(has_dn)
-            def _():
-                up_copy(p, t).wait_recv()
-                add_in(p, t, (BP[p], UP[p]))
-
-            @pl.when(z == 0)
-            def _():
-                add_in(p, t, (BP[p],))
-
-            up_copy(p, t).start()
-
-        @pl.when(n >= Z - 1 - z)
+            send(Z - 1 + z - n, up_copy, UP[p])
+
+        @pl.when((n >= Z - 1 - z) & has_up)
         def _():
-            t = n - (Z - 1 - z)
-            sib_copy(p, t).wait_recv()
-
-            @pl.when(has_up)
-            def _():
-                dn_copy(p, t).wait_recv()
-                add_in(p, t, (BP[p], NP[p]))
-
-            @pl.when(z == Z - 1)
-            def _():
-                add_in(p, t, (BP[p],))
-
-            dn_copy(p, t).start()
+            send(n - (Z - 1 - z), dn_copy, NP[p])
 
     def finish(p):
         fs, fin = ((FG, RG), (FD, RD))[p]
         sib_copy(p, z).wait_recv()
-        for e in range(E):
+        for j in list(range(1, E)) + [0]:
+            e = peer(j)
             fs[e] = DP[p][r, e].astype(F32) + BP[p][z, e].astype(F32)
 
-        @pl.when(has_dn)
-        def _():
-            up_copy(p, z).wait_recv()
-            fs[...] += UP[p][z].astype(F32)
-
-        @pl.when(has_up)
-        def _():
-            dn_copy(p, z).wait_recv()
-            fs[...] += NP[p][z].astype(F32)
-
-        for e in range(E):
-            DP[p][r, e] = fs[e].astype(BF16)
-        for j in range(1, E):
-            start(12 - p, j, DP[p].at[r, peer(j)], fin.at[q])
+            @pl.when(has_dn)
+            def _():
+                up_copy(p, z, e).wait_recv()
+                fs[e] += UP[p][z, e].astype(F32)
+
+            @pl.when(has_up)
+            def _():
+                dn_copy(p, z, e).wait_recv()
+                fs[e] += NP[p][z, e].astype(F32)
+
+            if j:
+                DP[p][r, e] = fs[e].astype(BF16)
+                start(12 - p, j, DP[p].at[r, e], fin.at[q])
 
     def place(p):
         cols, fs, fin = ((slice(0, H2), FG, RG), (slice(H2, 3 * H), FD, RD))[p]
@@ -387,29 +411,31 @@
         DX[:, s] = tot.astype(BF16).reshape(E, T, S)
         for j in range(1, E):
             copy_to(10, j, DX.at[peer(j), s], dx_out.at[:, span(s, q)]).start()
-        dx_out[:, span(s, q)] = DX[q, s]
+        pltpu.make_async_copy(DX.at[q, s], dx_out.at[:, span(s, q)], loc.at[4]).start()
         return carry
 
     spread(1)
     for i in range(Z):
         grads(1, i)
-    if Z > 1:
-        chain(1, 0)
+        if i:
+            chain_ends(1, i - 1)
     spread(0)
     for i in range(Z):
         grads(0, i)
-        if i == min(1, Z - 1) and Z > 2:
+        if i:
+            chain_ends(0, i - 1)
+        if i == Z // 2 and Z > 2:
             chain(1, 1)
-    if Z > 1:
-        chain(0, 0)
     for n in range(2, Z - 1):
         chain(1, n)
         if n < Z - 2:
             chain(0, n - 1)
+    if Z > 2:
+        chain(0, max(1, Z - 3))
     lax.fori_loop(0, R, input_rows, 0)
     for j in range(1, E):
         sent.append(copy_to(10, j, DX.at[q], DX.at[q]))
-    for n in range(max(1, Z - 3), Z - 1):
+    for n in range(max(1, Z - 3) + 1, Z - 1):
         chain(0, n)
     finish(1)
     finish(0)
@@ -417,29 +443,36 @@
     place(0)
     for j in range(1, E):
         got(10, j, DX.at[peer(j)])
+    pltpu.make_async_copy(DX.at[q], DX.at[q], loc.at[4]).wait()
 
     for d in sent:
         d.wait_send()
     for p in range(2):
         for t in range(Z):
-            w_copy(p, 2, t).wait_send()
             sib_copy(p, t).wait_send()
 
-            @pl.when((t <= z) & has_up)
-            def _():
-                w_copy(p, 0, t).wait_send()
-
-            @pl.when((t >= z) & has_dn)
-            def _():
-                w_copy(p, 1, t).wait_send()
-
-            @pl.when(t > z)
-            def _():
-                up_copy(p, t).wait_send()
-
-            @pl.when(t < z)
-            def _():
-                dn_copy(p, t).wait_send()
+            def left(e, carry):
+                w_copy(p, 2, t, e).wait_send()
+
+                @pl.when((t <= z) & has_up)
+                def _():
+                    w_copy(p, 0, t, e).wait_send()
+
+                @pl.when((t >= z) & has_dn)
+                def _():
+                    w_copy(p, 1, t, e).wait_send()
+
+                @pl.when(t > z)
+                def _():
+                    up_copy(p, t, e).wait_send()
+
+                @pl.when(t < z)
+                def _():
+                    dn_copy(p, t, e).wait_send()
+
+                return carry
+
+            lax.fori_loop(0, E, left, 0)
 
 
 def by_width(tokens, grad_out, gates, expert_ids, w_all, touched):
@@ -454,7 +487,7 @@
         touched[0, 0].reshape(R, E).T.astype(F32)[:, :, None], (E, R, 128)
     )
     vm = pl.BlockSpec(memory_space=pltpu.VMEM)
-    hbm = pl.BlockSpec(memory_space=pl.ANY)
+    hbm = pl.BlockSpec(memory_space=pltpu.HBM)
     dma = pltpu.SemaphoreType.DMA
 
     def two(*lead, kind=BF16, times=1):
@@ -467,8 +500,8 @@
             jax.ShapeDtypeStruct((T, D), BF16),
             jax.ShapeDtypeStruct((E, S, 3 * H), F32),
         ),
-        in_specs=[hbm] * 2 + [vm] * 4,
-        out_specs=(vm, vm),
+        in_specs=[hbm] * 3 + [vm] * 3,
+        out_specs=(hbm, vm),
         scratch_shapes=[wide, wide, pltpu.VMEM((E, T, 128), BF16), pltpu.VMEM((E, R, 128), F32)]
         + two(R, E, S)
         + two(E * T, kind=F32, times=E)
@@ -486,13 +519,13 @@
         + [
             dma((13, E)),
             dma((13, E)),
-            dma((2, R)),
-            dma((2, 3, Z)),
+            dma((2, R, E)),
+            dma((2, 3, Z, E)),
             dma((2, Z)),
             dma((2, Z)),
-            dma((2, 2, Z)),
-            dma((2, 2, Z)),
-            dma((2,)),
+            dma((2, 2, Z, E)),
+            dma((2, 2, Z, E)),
+            dma((5,)),
         ],
         compiler_params=pltpu.CompilerParams(
             collective_id=0, has_side_effects=True, vmem_limit_bytes=52 * 1024 * 1024

time: 97.8 us -> 93.7 us (0.958); the launches traced: 96.4 us -> 93.5 us
  Pallas kernels: 89.1 us -> 86.1 us
    pallas_call x1, Pallas kernels: 89.1 us -> 86.1 us  [by_width(): pl.pallas_call(functools.partial(kernel, R, E, T, S, H), out_shape=(jax.S...]
where the time goes in v3:
time: 93.7 us; the launch traced here: 93.5 us
  Pallas kernels  86.1 us (92%)
  local copies, waits for them, and re-layouts  6.64 us (7%)
    pallas_call x1, Pallas kernels, by_width(): pl.pallas_call(functools.partial(kernel, R, E, T, S, H), out_shape=(jax.S...  86.1 us
    unnamed x11, local copies, waits for them, and re-layouts  6.25 us

profile of v3, /device:TPU:8, one launch (start us, length us, event | category | flops | bytes accessed | tf_op | source)
XLA Modules:
  0.0 93.5 jit_solution(1917818502198382428)
XLA Ops:
  0.6 0.0 copy-start.2
  0.6 0.7 copy-done.2
  1.3 0.0 copy-start.3
  1.3 0.6 copy-done.3
  2.0 0.1 convert_element_type.16
  2.1 0.1 copy.15
  2.2 0.1 broadcast_in_dim.2.tm_ref
  2.2 0.1 copy.14
  2.4 0.0 copy-start.1
  2.4 0.7 copy-done.1
  3.0 0.1 copy.16.gate_ref
  3.2 0.0 copy-start
  3.2 1.0 %copy-done = bf16[1,512,384]{2,1,0:T(8,128)(2,1)S(1)} copy-done((bf16[1,512,384]{2,1,0:T(8,128)(2,1)S(1)}, bf16[1,512,384]{2,1,0:T(8,128)(2,1)}, u32[]{:S(2)}) %copy-start) | copy-done | bytes 393240
  4.2 86.1 %shard_map.77 = (bf16[128,4096]{1,0:T(8,128)(2,1)}, f32[4,128,384]{2,1,0:T(8,128)S(1)}) custom-call(bf16[128,4096]{1,0:T(8,128)(2,1)} %x_ref.1, bf16[128,4096]{1,0:T(8,128)(2,1)} %g_ref.1, bf16[4,128,384]{2,1,0:T(8,128)(2,1)S(1)} %bitcast.4, bf16[128,128]{1,0:T(8,128)(2,1)S(1)} %pad.4.id_ref, f32[4,8,128]{2,1,0:T(8,128)S(1)} %broadcast_in_dim.2.tm_ref, ...), custom_call_target="tpu_custom_call" | custom-call | tf_op jit(solution)/shard_map/pallas_call | solution.py:497
  90.3 2.3 %copy.19 = bf16[128,4096]{1,0:T(8,128)(2,1)} copy(bf16[128,4096]{1,0:T(8,128)(2,1)} %get-tuple-element.8) | data formatting | bytes 2097152
  92.6 0.9 copy.20
  (3 shorter events, 0.0 us)
Async XLA Ops:
  0.6 0.7 copy-start.2
  1.3 0.7 copy-start.3
  2.4 0.7 copy-start.1
  3.2 1.0 %copy-start = (bf16[1,512,384]{2,1,0:T(8,128)(2,1)S(1)}, bf16[1,512,384]{2,1,0:T(8,128)(2,1)}, u32[]{:S(2)}) copy-start(bf16[1,512,384]{2,1,0:T(8,128)(2,1)} %param.10) | copy-start | bytes 1179652

commit v4 on v3

--- a/solution.py
+++ b/solution.py
@@ -26,7 +26,7 @@
     R, E, T, S, H,
     x_ref, g_ref, w_ref, id_ref, tm_ref, gate_ref,
     dx_out, dw_out,
-    X, Y, IDS, TM, WG, WD, CG, CD, PG, PD, QG, QD, AG, AD, GU, HD, DX,
+    X, Y, XT, YT, IDS, TM, WG, WD, CG, CD, PG, PD, QG, QD, AG, AD, GU, HD, DX,
     DG, DD, BG, BD, UG, UD, NG, ND, FG, FD, RG, RD,
     a2s, a2r, wr, ws, bs, br, us, ur, loc,
 ):
@@ -210,6 +210,13 @@
                 w_slot(p, 2 * zz + 1 - c)
                 project(p, 2 * zz + 1 - c)
 
+    def turn(src, dst):
+        def body(s, carry):
+            dst[s] = src[:, s].reshape(E * T, S).T
+            return carry
+
+        lax.fori_loop(0, R, body, 0)
+
     w_first(0)
     w_first(1)
     for j in range(1, E):
@@ -217,18 +224,14 @@
         got(3, j, TM.at[peer(j)])
     if Z > 1:
         w_forward(0, 1)
-        w_forward(1, 1)
     pltpu.make_async_copy(X.at[q], X.at[q], loc.at[0]).wait()
     for j in range(1, E):
         got(4, j, X.at[peer(j)])
-    project_at(0, 0)
-    for d in range(2, Z):
-        w_forward(0, d)
+    for d in range(1, Z):
+        if d > 1:
+            w_forward(0, d)
         project_at(0, d - 1)
-        if d < Z - 1:
-            w_forward(1, d)
-    if Z > 1:
-        project_at(0, Z - 1)
+    project_at(0, Z - 1)
 
     def pairs(p):
         wid, acc, buf, dst = ((H2, CG, PG, QG), (H, CD, PD, QD))[p]
@@ -252,35 +255,52 @@
             tot = tot + dst[peer(j), :, k * wid : (k + 1) * wid].astype(F32)
         return tot
 
+    acts = []
+
+    def hidden():
+        for j in range(1, E):
+            got(6, j, QG.at[peer(j)])
+        for k in range(2):
+            tot = pair_sum(0, k)
+            silu_val, silu_slope = silu_terms(tot[:, :H])
+            up_pre, gate = tot[:, H:], gate_ref[:, k : k + 1]
+            acts.append((gate * up_pre * silu_slope, gate * silu_val))
+            AD[q, :, k * H : (k + 1) * H] = (gate * (silu_val * up_pre)).astype(BF16)
+        for j in range(1, E):
+            start(8, j, AD.at[q], AD.at[q])
+
+    def gate_up():
+        for j in range(1, E):
+            got(7, j, QD.at[peer(j)])
+        for k in range(2):
+            hid_grad = pair_sum(1, k)
+            AG[q, :, k * H2 : k * H2 + H] = (hid_grad * acts[k][0]).astype(BF16)
+            AG[q, :, k * H2 + H : (k + 1) * H2] = (hid_grad * acts[k][1]).astype(BF16)
+        for j in range(1, E):
+            start(9, j, AG.at[q], AG.at[q])
+
     pairs(0)
+    if Z > 1:
+        w_forward(1, 1)
     pltpu.make_async_copy(Y.at[q], Y.at[q], loc.at[1]).wait()
     for j in range(1, E):
         got(5, j, Y.at[peer(j)])
-    for d in range(Z - 1):
-        project_at(1, d)
-    if Z > 2:
-        w_forward(1, Z - 1)
-    project_at(1, Z - 1)
+    project_at(1, 0)
+    for d in range(2, Z):
+        w_forward(1, d)
+        if d == 2:
+            turn(X, XT)
+            turn(Y, YT)
+        project_at(1, d - 1)
+        if d == 2:
+            hidden()
+    if Z > 1:
+        project_at(1, Z - 1)
+    if Z <= 2:
+        turn(X, XT)
+        turn(Y, YT)
+        hidden()
     pairs(1)
-    for j in range(1, E):
-        got(6, j, QG.at[peer(j)])
-    acts = []
-    for k in range(2):
-        tot = pair_sum(0, k)
-        silu_val, silu_slope = silu_terms(tot[:, :H])
-        up_pre, gate = tot[:, H:], gate_ref[:, k : k + 1]
-        acts.append((gate * up_pre * silu_slope, gate * silu_val))
-        AD[q, :, k * H : (k + 1) * H] = (gate * (silu_val * up_pre)).astype(BF16)
-    for j in range(1, E):
-        start(8, j, AD.at[q], AD.at[q])
-    for j in range(1, E):
-        got(7, j, QD.at[peer(j)])
-    for k in range(2):
-        hid_grad = pair_sum(1, k)
-        AG[q, :, k * H2 : k * H2 + H] = (hid_grad * acts[k][0]).astype(BF16)
-        AG[q, :, k * H2 + H : (k + 1) * H2] = (hid_grad * acts[k][1]).astype(BF16)
-    for j in range(1, E):
-        start(9, j, AG.at[q], AG.at[q])
 
     def spread(p):
         wid, src, dst = ((H2, AG, GU), (H, AD, HD))[p]
@@ -299,13 +319,19 @@
 
     DP, BP, UP, NP = (DG, DD), (BG, BD), (UG, UD), (NG, ND)
 
-    def weight_rows(p, s):
-        src, wid, act = ((X, H2, GU), (Y, H, HD))[p]
-        v = contract_rows(src[:, s].reshape(E * T, S), act[...])
-        for e in range(E):
-            m = TM[e, pl.ds(s, 1), :]
-            for h in range(0, wid, H):
-                DP[p][s, e, :, h : h + H] = (v[:, e * wid + h : e * wid + h + H] * m).astype(BF16)
+    def weight_rows(p, t):
+        src, wid, act = ((XT, H2, GU), (YT, H, HD))[p]
+        rows = src[pl.ds(2 * t, 2)].reshape(2 * S, E * T)
+        step = min(E * wid, H2)
+        for n in range(0, E * wid, step):
+            v = jnp.dot(rows, act[:, n : n + step], preferred_element_type=F32)
+            for h in range(n, n + step, H):
+                e, col = h // wid, h % wid
+                for half in range(2):
+                    s = 2 * t + half
+                    m = TM[e, pl.ds(s, 1), :]
+                    part = v[half * S : (half + 1) * S, h - n : h - n + H]
+                    DP[p][s, e, :, col : col + H] = (part * m).astype(BF16)
 
     def sib_copy(p, t):
         return rcopy(DP[p].at[2 * t + 1 - c], BP[p].at[t], bs.at[p, t], br.at[p, t], sib)
@@ -320,9 +346,8 @@
 
     def grads(p, i):
         t = jnp.where(z < (Z + 1) // 2, Z - 1 - i, i)
-        weight_rows(p, 2 * t + 1 - c)
+        weight_rows(p, t)
         sib_copy(p, t).start()
-        weight_rows(p, 2 * t + c)
 
     def add_in(p, t, e, others):
         tot = DP[p][2 * t + c, e].astype(F32)
@@ -419,13 +444,15 @@
         grads(1, i)
         if i:
             chain_ends(1, i - 1)
+        if i == min(1, Z - 1):
+            gate_up()
+    if Z > 2:
+        chain(1, 1)
     spread(0)
     for i in range(Z):
         grads(0, i)
         if i:
             chain_ends(0, i - 1)
-        if i == Z // 2 and Z > 2:
-            chain(1, 1)
     for n in range(2, Z - 1):
         chain(1, n)
         if n < Z - 2:
@@ -494,6 +521,7 @@
         return [pltpu.VMEM(lead + (times * 2 * H,), kind), pltpu.VMEM(lead + (times * H,), kind)]
 
     wide = pltpu.VMEM((E, R, T, S), BF16)
+    tall = pltpu.VMEM((R, S, E * T), BF16)
     dx, dw = pl.pallas_call(
         functools.partial(kernel, R, E, T, S, H),
         out_shape=(
@@ -502,7 +530,7 @@
         ),
         in_specs=[hbm] * 3 + [vm] * 3,
         out_specs=(hbm, vm),
-        scratch_shapes=[wide, wide, pltpu.VMEM((E, T, 128), BF16), pltpu.VMEM((E, R, 128), F32)]
+        scratch_shapes=[wide, wide, tall, tall, pltpu.VMEM((E, T, 128), BF16), pltpu.VMEM((E, R, 128), F32)]
         + two(R, E, S)
         + two(E * T, kind=F32, times=E)
         + two(E, T, times=2)

time: 93.7 us -> 94.8 us (1.012)
  Pallas kernels: 86.1 us -> 87.3 us
    pallas_call x1, Pallas kernels: 86.1 us -> 87.3 us  [by_width(): pl.pallas_call(functools.partial(kernel, R, E, T, S, H), out_shape=(jax.S...]
where the time goes in v4:
time: 94.8 us; the launch traced here: 94.6 us
  Pallas kernels  87.3 us (92%)
  local copies, waits for them, and re-layouts  6.64 us (7%)
    pallas_call x1, Pallas kernels, by_width(): pl.pallas_call(functools.partial(kernel, R, E, T, S, H), out_shape=(jax.S...  87.3 us
    unnamed x11, local copies, waits for them, and re-layouts  6.25 us

profile of v4, /device:TPU:8, one launch (start us, length us, event | category | flops | bytes accessed | tf_op | source)
XLA Modules:
  0.0 94.6 jit_solution(12016441328753000101)
XLA Ops:
  0.6 0.0 copy-start.2
  0.6 0.7 copy-done.2
  1.3 0.0 copy-start.3
  1.3 0.6 copy-done.3
  2.0 0.1 convert_element_type.16
  2.1 0.1 copy.15
  2.2 0.1 broadcast_in_dim.2.tm_ref
  2.2 0.1 copy.14
  2.4 0.0 copy-start.1
  2.4 0.7 copy-done.1
  3.0 0.1 copy.16.gate_ref
  3.2 0.0 copy-start
  3.2 1.0 %copy-done = bf16[1,512,384]{2,1,0:T(8,128)(2,1)S(1)} copy-done((bf16[1,512,384]{2,1,0:T(8,128)(2,1)S(1)}, bf16[1,512,384]{2,1,0:T(8,128)(2,1)}, u32[]{:S(2)}) %copy-start) | copy-done | bytes 393240
  4.2 87.3 %shard_map.77 = (bf16[128,4096]{1,0:T(8,128)(2,1)}, f32[4,128,384]{2,1,0:T(8,128)S(1)}) custom-call(bf16[128,4096]{1,0:T(8,128)(2,1)} %x_ref.1, bf16[128,4096]{1,0:T(8,128)(2,1)} %g_ref.1, bf16[4,128,384]{2,1,0:T(8,128)(2,1)S(1)} %bitcast.4, bf16[128,128]{1,0:T(8,128)(2,1)S(1)} %pad.4.id_ref, f32[4,8,128]{2,1,0:T(8,128)S(1)} %broadcast_in_dim.2.tm_ref, ...), custom_call_target="tpu_custom_call" | custom-call | tf_op jit(solution)/shard_map/pallas_call | solution.py:525
  91.4 2.3 %copy.19 = bf16[128,4096]{1,0:T(8,128)(2,1)} copy(bf16[128,4096]{1,0:T(8,128)(2,1)} %get-tuple-element.8) | data formatting | bytes 2097152
  93.7 0.9 copy.20
  (3 shorter events, 0.0 us)
Async XLA Ops:
  0.6 0.7 copy-start.2
  1.3 0.7 copy-start.3
  2.4 0.7 copy-start.1
  3.2 1.0 %copy-start = (bf16[1,512,384]{2,1,0:T(8,128)(2,1)S(1)}, bf16[1,512,384]{2,1,0:T(8,128)(2,1)}, u32[]{:S(2)}) copy-start(bf16[1,512,384]{2,1,0:T(8,128)(2,1)} %param.10) | copy-start | bytes 1179652

commit v5 on v3

--- a/solution.py
+++ b/solution.py
@@ -24,9 +24,9 @@
 
 def kernel(
     R, E, T, S, H,
-    x_ref, g_ref, w_ref, id_ref, tm_ref, gate_ref,
+    x_ref, g_ref, w_ref, id_ref, touch_ref, gate_ref,
     dx_out, dw_out,
-    X, Y, IDS, TM, WG, WD, CG, CD, PG, PD, QG, QD, AG, AD, GU, HD, DX,
+    X, Y, IDS, TM, IDV, GTV, GATE, WG, WD, CG, CD, PG, PD, QG, QD, AG, AD, GU, HD, DX,
     DG, DD, BG, BD, UG, UD, NG, ND, FG, FD, RG, RD,
     a2s, a2r, wr, ws, bs, br, us, ur, loc,
 ):
@@ -53,6 +53,13 @@
 
     pltpu.make_async_copy(w_ref.at[q, :, :H2], WG.at[r, q], loc.at[2]).start()
     pltpu.make_async_copy(w_ref.at[q, :, H2:], WD.at[r, q], loc.at[3]).start()
+    small = (
+        pltpu.make_async_copy(id_ref, IDV, loc.at[5]),
+        pltpu.make_async_copy(gate_ref, GTV, loc.at[6]),
+        pltpu.make_async_copy(touch_ref, TM.at[q], loc.at[7]),
+    )
+    for d in small:
+        d.start()
     lax.fori_loop(0, R, own_cols, 0)
 
     barrier = pltpu.get_barrier_semaphore()
@@ -167,9 +174,18 @@
         start(1, j, w_ref.at[peer(j), :, H2:], WD.at[r, q])
     own_w[1].wait()
     w_own(1)
-    for j in range(1, E):
-        start(2, j, id_ref, IDS.at[q])
-        start(3, j, tm_ref.at[peer(j)], TM.at[q])
+    for d in small:
+        d.wait()
+
+    def columns(ref):
+        first = lax.broadcasted_iota(jnp.int32, (T, T), 0) == 0
+        return jnp.where(first, ref[0:1].astype(F32), ref[1:2].astype(F32)).T
+
+    IDS[q] = columns(IDV).astype(BF16)
+    GATE[...] = columns(GTV)
+    for j in range(1, E):
+        start(2, j, IDS.at[q], IDS.at[q])
+        start(3, j, TM.at[q], TM.at[q])
 
     def send_cols(kind, src, buf):
         def body(s, carry):
@@ -183,8 +199,6 @@
 
     send_cols(4, x_ref, X)
     send_cols(5, g_ref, Y)
-    IDS[q] = id_ref[...]
-    TM[q] = tm_ref[q]
 
     def project(p, s, first=False):
         src, wid, acc = ((X, H2, CG), (Y, H, CD))[p]
@@ -268,7 +282,7 @@
     for k in range(2):
         tot = pair_sum(0, k)
         silu_val, silu_slope = silu_terms(tot[:, :H])
-        up_pre, gate = tot[:, H:], gate_ref[:, k : k + 1]
+        up_pre, gate = tot[:, H:], GATE[:, k : k + 1]
         acts.append((gate * up_pre * silu_slope, gate * silu_val))
         AD[q, :, k * H : (k + 1) * H] = (gate * (silu_val * up_pre)).astype(BF16)
     for j in range(1, E):
@@ -303,7 +317,9 @@
         src, wid, act = ((X, H2, GU), (Y, H, HD))[p]
         v = contract_rows(src[:, s].reshape(E * T, S), act[...])
         for e in range(E):
-            m = TM[e, pl.ds(s, 1), :]
+            row = TM[e]
+            here = lax.broadcasted_iota(jnp.int32, row.shape, 1) == s * E + q
+            m = jnp.sum(jnp.where(here, row, 0), axis=1, keepdims=True).astype(F32)
             for h in range(0, wid, H):
                 DP[p][s, e, :, h : h + H] = (v[:, e * wid + h : e * wid + h + H] * m).astype(BF16)
 
@@ -475,6 +491,20 @@
             lax.fori_loop(0, E, left, 0)
 
 
+def hand_on(dx_ref, dw_ref, dx_out, dw_out, sems):
+    n = dw_ref.shape[0]
+    rows = dx_ref.shape[0] // n
+    copies = []
+    for i in range(n):
+        part = pl.ds(i * rows, rows)
+        copies.append(pltpu.make_async_copy(dx_ref.at[part], dx_out.at[part], sems.at[0, i]))
+        copies.append(pltpu.make_async_copy(dw_ref.at[i], dw_out.at[i], sems.at[1, i]))
+    for d in copies:
+        d.start()
+    for d in copies:
+        d.wait()
+
+
 def by_width(tokens, grad_out, gates, expert_ids, w_all, touched):
     E, R = lax.axis_size("exp"), lax.axis_size("rep")
     T, D = tokens.shape
@@ -482,10 +512,7 @@
     H = w_all.shape[2] // 3
     Z = R // 2
     w = w_all[0].reshape(E, S, 3 * H)
-    ids = jnp.pad(expert_ids.astype(BF16), ((0, 0), (0, 128 - 2)))
-    tm = jnp.broadcast_to(
-        touched[0, 0].reshape(R, E).T.astype(F32)[:, :, None], (E, R, 128)
-    )
+    blocks = touched.shape[2]
     vm = pl.BlockSpec(memory_space=pltpu.VMEM)
     hbm = pl.BlockSpec(memory_space=pltpu.HBM)
     dma = pltpu.SemaphoreType.DMA
@@ -500,9 +527,10 @@
             jax.ShapeDtypeStruct((T, D), BF16),
             jax.ShapeDtypeStruct((E, S, 3 * H), F32),
         ),
-        in_specs=[hbm] * 3 + [vm] * 3,
-        out_specs=(hbm, vm),
-        scratch_shapes=[wide, wide, pltpu.VMEM((E, T, 128), BF16), pltpu.VMEM((E, R, 128), F32)]
+        in_specs=[hbm] * 6,
+        out_specs=(vm, vm),
+        scratch_shapes=[wide, wide, pltpu.VMEM((E, T, 128), BF16), pltpu.VMEM((E, 1, blocks), jnp.int32)]
+        + [pltpu.VMEM((2, T), jnp.int32), pltpu.VMEM((2, T), F32), pltpu.VMEM((T, T), F32)]
         + two(R, E, S)
         + two(E * T, kind=F32, times=E)
         + two(E, T, times=2)
@@ -525,12 +553,24 @@
             dma((2, Z)),
             dma((2, 2, Z, E)),
             dma((2, 2, Z, E)),
-            dma((5,)),
+            dma((8,)),
         ],
         compiler_params=pltpu.CompilerParams(
-            collective_id=0, has_side_effects=True, vmem_limit_bytes=52 * 1024 * 1024
+            collective_id=0, has_side_effects=True, vmem_limit_bytes=60 * 1024 * 1024
         ),
-    )(tokens, grad_out, w, ids, tm, gates)
+    )(tokens, grad_out, w, expert_ids.T, touched[0], gates.T)
+    some = pl.BlockSpec(memory_space=pl.ANY)
+    dx, dw = pl.pallas_call(
+        hand_on,
+        out_shape=(
+            jax.ShapeDtypeStruct((T, D), BF16),
+            jax.ShapeDtypeStruct((E, S, 3 * H), F32),
+        ),
+        in_specs=[some] * 2,
+        out_specs=(hbm, hbm),
+        scratch_shapes=[dma((2, E))],
+        compiler_params=pltpu.CompilerParams(vmem_limit_bytes=60 * 1024 * 1024),
+    )(dx, dw)
     return dx, dw.reshape(1, E * S, 3 * H)
 
 
@@ -620,7 +660,7 @@
     R, E = lax.axis_size("rep"), lax.axis_size("exp")
     share, rest = divmod(tokens.shape[1], R * E)
     fits = rest == 0 and share == 128 and R % 16 in (0, 8)
-    fits = fits and tokens.shape[0] % 16 == 0 and w_all.shape[2] == 3 * 128
+    fits = fits and tokens.shape[0] == 128 and w_all.shape[2] == 3 * 128
     plan = by_width if fits else by_expert
     return plan(tokens, grad_out, gates, expert_ids, w_all, touched)
 

time: 93.7 us -> 145 us (1.55)
  Pallas kernels: 86.1 us -> 144 us
  local copies, waits for them, and re-layouts: 6.64 us -> 0 us
    pallas_call x0 -> x1, Pallas kernels: none -> 56.8 us  [by_width(): pl.pallas_call(hand_on, out_shape=(jax.ShapeDtypeStruct((T, D), BF16), ja...]
    unnamed x11 -> x0, local copies, waits for them, and re-layouts: 6.25 us -> none
where the time goes in v5:
time: 145 us
  Pallas kernels  144 us (99%)
    pallas_call x1, Pallas kernels, by_width(): pl.pallas_call(functools.partial(kernel, R, E, T, S, H), out_shape=(jax.S...  87.5 us
    pallas_call x1, Pallas kernels, by_width(): pl.pallas_call(hand_on, out_shape=(jax.ShapeDtypeStruct((T, D), BF16), ja...  56.8 us

profile of v5, /device:TPU:8, one launch (start us, length us, event | category | flops | bytes accessed | tf_op | source)
XLA Modules:
  0.0 144.9 jit_solution(2762204334587978948)
XLA Ops:
  0.6 87.5 %shard_map.77 = (bf16[128,4096]{1,0:T(8,128)(2,1)}, f32[4,128,384]{2,1,0:T(8,128)}) custom-call(bf16[128,4096]{1,0:T(8,128)(2,1)} %x_ref.1, bf16[128,4096]{1,0:T(8,128)(2,1)} %g_ref.1, bf16[4,128,384]{2,1,0:T(8,128)(2,1)} %bitcast.5, s32[2,128]{1,0:T(2,128)} %bitcast.6, s32[1,32]{1,0:T(1,128)} %bitcast.8, f32[2,128]{1,0:T(2,128)} %bitcast.7), custom_call_target="tpu_custom_call" | custom-call | tf_op jit(solution)/shard_map/pallas_call | solution.py:524
  88.2 56.8 %shard_map.78 = (bf16[128,4096]{1,0:T(8,128)(2,1)}, f32[4,128,384]{2,1,0:T(8,128)}) custom-call(bf16[128,4096]{1,0:T(8,128)(2,1)} %get-tuple-element.6.dx_ref, f32[4,128,384]{2,1,0:T(8,128)} %get-tuple-element.7.dw_ref), custom_call_target="tpu_custom_call" | custom-call | tf_op jit(solution)/shard_map/pallas_call | solution.py:563

commit v6 on v5

--- a/solution.py
+++ b/solution.py
@@ -491,18 +491,9 @@
             lax.fori_loop(0, E, left, 0)
 
 
-def hand_on(dx_ref, dw_ref, dx_out, dw_out, sems):
-    n = dw_ref.shape[0]
-    rows = dx_ref.shape[0] // n
-    copies = []
-    for i in range(n):
-        part = pl.ds(i * rows, rows)
-        copies.append(pltpu.make_async_copy(dx_ref.at[part], dx_out.at[part], sems.at[0, i]))
-        copies.append(pltpu.make_async_copy(dw_ref.at[i], dw_out.at[i], sems.at[1, i]))
-    for d in copies:
-        d.start()
-    for d in copies:
-        d.wait()
+def hand_on(dx_ref, dw_ref, dx_out, dw_out):
+    dx_out[...] = dx_ref[...]
+    dw_out[...] = dw_ref[...]
 
 
 def by_width(tokens, grad_out, gates, expert_ids, w_all, touched):
@@ -559,16 +550,19 @@
             collective_id=0, has_side_effects=True, vmem_limit_bytes=60 * 1024 * 1024
         ),
     )(tokens, grad_out, w, expert_ids.T, touched[0], gates.T)
-    some = pl.BlockSpec(memory_space=pl.ANY)
+    parts = [
+        pl.BlockSpec((T // E, D), lambda i: (i, 0)),
+        pl.BlockSpec((1, S, 3 * H), lambda i: (i, 0, 0)),
+    ]
     dx, dw = pl.pallas_call(
         hand_on,
+        grid=(E,),
         out_shape=(
             jax.ShapeDtypeStruct((T, D), BF16),
             jax.ShapeDtypeStruct((E, S, 3 * H), F32),
         ),
-        in_specs=[some] * 2,
-        out_specs=(hbm, hbm),
-        scratch_shapes=[dma((2, E))],
+        in_specs=parts,
+        out_specs=parts,
         compiler_params=pltpu.CompilerParams(vmem_limit_bytes=60 * 1024 * 1024),
     )(dx, dw)
     return dx, dw.reshape(1, E * S, 3 * H)
@@ -659,7 +653,7 @@
 def per_device(tokens, grad_out, gates, expert_ids, w_all, touched):
     R, E = lax.axis_size("rep"), lax.axis_size("exp")
     share, rest = divmod(tokens.shape[1], R * E)
-    fits = rest == 0 and share == 128 and R % 16 in (0, 8)
+    fits = rest == 0 and share == 128 and tokens.shape[0] % (16 * E) == 0
     fits = fits and tokens.shape[0] == 128 and w_all.shape[2] == 3 * 128
     plan = by_width if fits else by_expert
     return plan(tokens, grad_out, gates, expert_ids, w_all, touched)

time: 145 us -> 92 us (0.63)
  Pallas kernels: 144 us -> 91.2 us
    pallas_call x1, Pallas kernels: 56.8 us -> 3.64 us  [by_width(): pl.pallas_call(hand_on, grid=(E,), out_shape=(jax.ShapeDtypeStruct((T, D)...]
where the time goes in v6:
time: 92 us; the launch traced here: 91.8 us
  Pallas kernels  91.2 us (99%)
    pallas_call x1, Pallas kernels, by_width(): pl.pallas_call(functools.partial(kernel, R, E, T, S, H), out_shape=(jax.S...  87.5 us
    pallas_call x1, Pallas kernels, by_width(): pl.pallas_call(hand_on, grid=(E,), out_shape=(jax.ShapeDtypeStruct((T, D)...  3.64 us

profile of v6, /device:TPU:8, one launch (start us, length us, event | category | flops | bytes accessed | tf_op | source)
XLA Modules:
  0.0 91.8 jit_solution(11737034561258592657)
XLA Ops:
  0.6 87.5 %shard_map.77 = (bf16[128,4096]{1,0:T(8,128)(2,1)}, f32[4,128,384]{2,1,0:T(8,128)}) custom-call(bf16[128,4096]{1,0:T(8,128)(2,1)} %x_ref.1, bf16[128,4096]{1,0:T(8,128)(2,1)} %g_ref.1, bf16[4,128,384]{2,1,0:T(8,128)(2,1)} %bitcast.5, s32[2,128]{1,0:T(2,128)} %bitcast.6, s32[1,32]{1,0:T(1,128)} %bitcast.8, f32[2,128]{1,0:T(2,128)} %bitcast.7), custom_call_target="tpu_custom_call" | custom-call | tf_op jit(solution)/shard_map/pallas_call | solution.py:515
  88.2 3.6 %shard_map.78 = (bf16[128,4096]{1,0:T(8,128)(2,1)}, f32[4,128,384]{2,1,0:T(8,128)}) custom-call(bf16[128,4096]{1,0:T(8,128)(2,1)} %get-tuple-element.6.dx_ref, f32[4,128,384]{2,1,0:T(8,128)} %get-tuple-element.7.dw_ref), custom_call_target="tpu_custom_call" | custom-call | tf_op jit(solution)/shard_map/pallas_call | solution.py:557
